TPU v7x, 512 devices: a whole 4x8x8 slice. The times are simulated.
512 devices in a mesh: blk: 32 (over x, y), layer: 16 (over z, core).
Axes of the slice: x: 4, y: 8, z: 8, core: 2. Of those that a mesh axis runs over, the one named last changes fastest.
Arguments:
- a_vals: float32 [16, 512, 6, 4096], P('layer', 'blk'), may hold values from -0.75 to 0.75
- a_cols: int32 [16, 512, 6], P('layer', 'blk'), may hold values from 0 to 31, all different within a row; in each aligned block of 16 rows (0 to 15, 16 to 31, ..., all dimensions but the last counted through in order) at most 6 rows name the same one
- b_vals: float32 [512, 4, 4096], P(('blk', 'layer')), may hold values from -6 to 6
- b_cols: int32 [512, 4], P(('blk', 'layer')), may hold values from 0 to 511, all different within a row
- c_cols: int32 [512, 16], P('blk'), may hold values from 0 to 511, all different within a row
- c_keep: int32 [512, 16], P('blk', 'layer'), may hold values 0 or 1
- c_vals: float32 [512, 16, 4096], P('blk', 'layer'), may hold values from -6 to 6
Outputs:
- x_next: float32 [512, 16, 4096], P('blk', 'layer')
Inputs may be any that keep to these rules, and one draw needn't show every extreme that they name: `a_cols`: in each layer every block row names 6 different inner indices; of the 16 block rows of one device at most 6 name the same inner index in one layer, and some inner index is named by exactly 6 of them. `b_cols`: each block row names 4 different block columns. `c_cols`: each block row names 16 different block columns.
All inputs are finite; a program needn't handle non-finite values. No bound on the sum of `c_keep` on one device may be relied on, other than what follows from the above.
Results may differ from a plain program's by a relative error of at most 0.0003.
Values sent between devices are 32-bit elements; how exact they have to be, the bound alone decides.
A program may use at most 128 MiB of HBM per device.

v0:
```python
import jax
import jax.numpy as jnp
from jax import lax
from jax.sharding import PartitionSpec as P

BLK = 64
CAP_MAX = 6


def shifted(value, axis, by):
    devices = lax.axis_size(axis)
    return lax.ppermute(value, axis, [(i, (i + by) % devices) for i in range(devices)])


def body(a_vals, a_cols, b_vals, b_cols, c_cols, c_keep, c_vals):
    left_store = a_vals[0]
    left_cols = a_cols[0]
    row_count, per_row, block_size = left_store.shape
    own_rows, per_brow = b_cols.shape
    slot_count = c_cols.shape[1]
    cycle_size = lax.axis_size("blk")
    capacity = min(CAP_MAX, row_count)
    myself = lax.axis_index("blk")
    left_flat = left_store.reshape(row_count * per_row, block_size)
    slot_range = jnp.arange(per_row, dtype=jnp.int32)
    row_range = jnp.arange(row_count, dtype=jnp.int32)
    cap_range = jnp.arange(capacity, dtype=jnp.int32)

    def forward(values, columns):
        return shifted((values, columns), "blk", 1)

    def deposit(totals, first_row, values, columns):
        count = values.shape[0]
        inner_rows = first_row + jnp.arange(count, dtype=jnp.int32)
        matches = left_cols[None, :, :] == inner_rows[:, None, None]
        holders = jnp.any(matches, axis=2)
        slot_index = jnp.sum(jnp.where(matches, slot_range, 0), axis=2)
        ranking = jnp.cumsum(holders.astype(jnp.int32), axis=1) - 1
        chosen = holders[:, :, None] & (ranking[:, :, None] == cap_range)
        active = jnp.any(chosen, axis=1)
        row_index = jnp.sum(jnp.where(chosen, row_range[None, :, None], 0), axis=1)
        slot_pick = jnp.sum(jnp.where(chosen, slot_index[:, :, None], 0), axis=1)
        left_blocks = left_flat[row_index * per_row + slot_pick].reshape(count, capacity, BLK, BLK)
        right_blocks = values.reshape(count, per_brow, BLK, BLK)
        products = jnp.einsum(
            "rcxy,rsyz->rcsxz", left_blocks, right_blocks, precision=lax.Precision.HIGHEST
        )
        wanted = c_cols[row_index]
        agrees = (columns[:, None, :, None] == wanted[:, :, None, :]) & active[:, :, None, None]
        row_hits = row_index[:, :, None] == row_range[None, None, :]
        landing = (row_hits[:, :, None, :, None] & agrees[:, :, :, None, :]).astype(jnp.float32)
        landing = landing.reshape(count * capacity * per_brow, row_count * slot_count)
        flat_products = products.reshape(count * capacity * per_brow, block_size)
        added = jnp.dot(
            landing.T,
            flat_products,
            precision=lax.Precision.HIGHEST,
            preferred_element_type=jnp.float32,
        )
        return totals + added.reshape(row_count, slot_count, block_size)

    totals = jnp.zeros((row_count, slot_count, block_size), jnp.float32)
    totals = deposit(totals, myself * own_rows, b_vals, b_cols)

    def advance(stride, carried):
        totals, ahead_vals, ahead_cols = carried
        ahead_vals, ahead_cols = forward(ahead_vals, ahead_cols)
        source = (myself - stride + cycle_size) % cycle_size * own_rows
        totals = deposit(totals, source, ahead_vals, ahead_cols)
        return (totals, ahead_vals, ahead_cols)

    totals = lax.fori_loop(1, cycle_size, advance, (totals, b_vals, b_cols))[0]
    summed = lax.psum_scatter(totals, "layer", scatter_dimension=1, tiled=True)
    keep = c_keep.astype(jnp.float32)[:, :, None]
    return keep * (1.5 * c_vals - 0.5 * summed)


def solution(mesh):
    in_specs = (
        P("layer", "blk", None, None),
        P("layer", "blk", None),
        P(("blk", "layer"), None, None),
        P(("blk", "layer"), None),
        P("blk", None),
        P("blk", "layer"),
        P("blk", "layer", None),
    )
    out_specs = P("blk", "layer", None)
    return jax.shard_map(body, mesh=mesh, in_specs=in_specs, out_specs=out_specs, check_vma=False)
```

profile of v0, /device:TPU:1, one launch (start us, length us, event | category | flops | bytes accessed | tf_op | source)
XLA Modules:
  0.0 669.7 jit_solution(13039027468093755733)
XLA Ops:
  12.0 3.7 copy.27
  19.3 3.8 fusion.17
  23.1 533.8 %while.21 = (s32[]{:T(128)}, f32[16,16,4096]{2,1,0:T(8,128)}, f32[1,4,4096]{2,1,0:T(4,128)S(1)}, s32[1,4]{1,0:T(1,128)S(1)}, s32[]{:T(128)}, /*index=5*/s32[1,16...) while((s32[]{:T(128)}, f32[16,16,4096]{2,1,0:T(8,128)}, ...), condition=%wide.region_13.14_spmd.clone.clone, body=%wide.region_6.13_spmd.clone.clone.sunk | while | flops 378546624 | bytes 11092250 | solution.py:72
  23.1 4.0 collective-permute-start.1
  36.4 5.9 convolution_add_fusion.2
  44.2 3.5 collective-permute-start
  53.5 5.9 convolution_add_fusion.2
  65.5 3.5 collective-permute-done
  70.6 5.9 convolution_add_fusion.2
  82.6 3.5 collective-permute-done
  87.8 5.9 convolution_add_fusion.2
  99.8 3.5 collective-permute-done
  104.9 5.9 convolution_add_fusion.2
  122.0 5.9 convolution_add_fusion.2
  134.0 3.5 collective-permute-done
  139.2 5.9 convolution_add_fusion.2
  151.2 3.5 collective-permute-done
  156.3 5.9 convolution_add_fusion.2
  173.4 5.9 convolution_add_fusion.2
  190.6 5.9 convolution_add_fusion.2
  207.7 5.9 convolution_add_fusion.2
  224.8 5.9 convolution_add_fusion.2
  242.0 5.9 convolution_add_fusion.2
  253.9 3.8 collective-permute-done
  259.4 5.9 convolution_add_fusion.2
  276.5 5.9 convolution_add_fusion.2
  293.7 5.9 convolution_add_fusion.2
  310.8 5.9 convolution_add_fusion.2
  327.9 5.9 convolution_add_fusion.2
  345.1 5.9 convolution_add_fusion.2
  362.2 5.9 convolution_add_fusion.2
  374.2 3.5 collective-permute-done
  379.3 5.9 convolution_add_fusion.2
  396.5 5.9 convolution_add_fusion.2
  413.6 5.9 convolution_add_fusion.2
  425.6 3.5 collective-permute-done
  430.7 5.9 convolution_add_fusion.2
  447.9 5.9 convolution_add_fusion.2
  465.0 5.9 convolution_add_fusion.2
  482.1 5.9 convolution_add_fusion.2
  499.3 5.9 convolution_add_fusion.2
  511.2 3.5 collective-permute-done
  516.4 5.9 convolution_add_fusion.2
  528.4 3.8 collective-permute-done
  533.8 5.9 convolution_add_fusion.2
  551.0 5.9 convolution_add_fusion.2
  556.9 6.5 copy.29
  564.1 96.6 %reduce-scatter.2.cloned.1.call-done = f32[16,1,4096]{2,0,1:T(8,128)} async-done(((f32[16,16,4096]{2,0,1:T(8,128)}), f32[16,1,4096]{2,0,1:T(8,128)}) %reduce-scatter.2.cloned.1.call-update) | async-done | bytes 262160 | tf_op jit(solution)/shard_map/reduce_scatter | solution.py:73
  (893 shorter events, 315.2 us)
Async XLA Ops:
  6.5 654.2 %reduce-scatter.2.cloned.1.call-start = ((), (), s32[]{:S(2)}) async-start(), calls=%async_computation.1 | async-start | bytes 4456448 | tf_op jit(solution)/shard_map/reduce_scatter | solution.py:73
  23.1 12.1 %collective-permute-start.1 = (f32[1,4,4096]{2,1,0:T(4,128)S(1)}, f32[1,4,4096]{2,1,0:T(4,128)S(1)}, u32[]{:S(2)}, u32[]{:S(2)}) collective-permute-start(f32[1,4,4096]{2,1,0:T(4,128)S(1)} %get-tuple-element.435), channel_id=1, source_target_pairs={{0,16},{16,32},{32,48},{48,64},{64,80},{80,96},{96,112},{112,128},... | collective-permute-start | bytes 196616 | tf_op jit(solution)/shard_map/while/body/eval_jaxpr/ppermute | solution.py:12
  42.3 10.0 %collective-permute-start.1 = (f32[1,4,4096]{2,1,0:T(4,128)S(1)}, f32[1,4,4096]{2,1,0:T(4,128)S(1)}, u32[]{:S(2)}, u32[]{:S(2)}) collective-permute-start(f32[1,4,4096]{2,1,0:T(4,128)S(1)} %get-tuple-element.435), channel_id=1, source_target_pairs={{0,16},{16,32},{32,48},{48,64},{64,80},{80,96},{96,112},{112,128},... | collective-permute-start | bytes 196616 | tf_op jit(solution)/shard_map/while/body/eval_jaxpr/ppermute | solution.py:12
  44.2 7.6 %collective-permute-start = (s32[1,4]{1,0:T(1,128)S(1)}, s32[1,4]{1,0:T(1,128)S(1)}, u32[]{:S(2)}, u32[]{:S(2)}) collective-permute-start(s32[1,4]{1,0:T(1,128)S(1)} %get-tuple-element.436), channel_id=1, source_target_pairs={{0,16},{16,32},{32,48},{48,64},{64,80},{80,96},{96,112},{112,128},... | collective-permute-start | bytes 56 | tf_op jit(solution)/shard_map/while/body/eval_jaxpr/ppermute | solution.py:12
  59.5 10.0 %collective-permute-start.1 = (f32[1,4,4096]{2,1,0:T(4,128)S(1)}, f32[1,4,4096]{2,1,0:T(4,128)S(1)}, u32[]{:S(2)}, u32[]{:S(2)}) collective-permute-start(f32[1,4,4096]{2,1,0:T(4,128)S(1)} %get-tuple-element.435), channel_id=1, source_target_pairs={{0,16},{16,32},{32,48},{48,64},{64,80},{80,96},{96,112},{112,128},... | collective-permute-start | bytes 196616 | tf_op jit(solution)/shard_map/while/body/eval_jaxpr/ppermute | solution.py:12
  61.4 7.6 %collective-permute-start = (s32[1,4]{1,0:T(1,128)S(1)}, s32[1,4]{1,0:T(1,128)S(1)}, u32[]{:S(2)}, u32[]{:S(2)}) collective-permute-start(s32[1,4]{1,0:T(1,128)S(1)} %get-tuple-element.436), channel_id=1, source_target_pairs={{0,16},{16,32},{32,48},{48,64},{64,80},{80,96},{96,112},{112,128},... | collective-permute-start | bytes 56 | tf_op jit(solution)/shard_map/while/body/eval_jaxpr/ppermute | solution.py:12
  76.6 10.0 %collective-permute-start.1 = (f32[1,4,4096]{2,1,0:T(4,128)S(1)}, f32[1,4,4096]{2,1,0:T(4,128)S(1)}, u32[]{:S(2)}, u32[]{:S(2)}) collective-permute-start(f32[1,4,4096]{2,1,0:T(4,128)S(1)} %get-tuple-element.435), channel_id=1, source_target_pairs={{0,16},{16,32},{32,48},{48,64},{64,80},{80,96},{96,112},{112,128},... | collective-permute-start | bytes 196616 | tf_op jit(solution)/shard_map/while/body/eval_jaxpr/ppermute | solution.py:12
  78.5 7.6 %collective-permute-start = (s32[1,4]{1,0:T(1,128)S(1)}, s32[1,4]{1,0:T(1,128)S(1)}, u32[]{:S(2)}, u32[]{:S(2)}) collective-permute-start(s32[1,4]{1,0:T(1,128)S(1)} %get-tuple-element.436), channel_id=1, source_target_pairs={{0,16},{16,32},{32,48},{48,64},{64,80},{80,96},{96,112},{112,128},... | collective-permute-start | bytes 56 | tf_op jit(solution)/shard_map/while/body/eval_jaxpr/ppermute | solution.py:12
  93.7 10.0 %collective-permute-start.1 = (f32[1,4,4096]{2,1,0:T(4,128)S(1)}, f32[1,4,4096]{2,1,0:T(4,128)S(1)}, u32[]{:S(2)}, u32[]{:S(2)}) collective-permute-start(f32[1,4,4096]{2,1,0:T(4,128)S(1)} %get-tuple-element.435), channel_id=1, source_target_pairs={{0,16},{16,32},{32,48},{48,64},{64,80},{80,96},{96,112},{112,128},... | collective-permute-start | bytes 196616 | tf_op jit(solution)/shard_map/while/body/eval_jaxpr/ppermute | solution.py:12
  110.9 10.0 %collective-permute-start.1 = (f32[1,4,4096]{2,1,0:T(4,128)S(1)}, f32[1,4,4096]{2,1,0:T(4,128)S(1)}, u32[]{:S(2)}, u32[]{:S(2)}) collective-permute-start(f32[1,4,4096]{2,1,0:T(4,128)S(1)} %get-tuple-element.435), channel_id=1, source_target_pairs={{0,16},{16,32},{32,48},{48,64},{64,80},{80,96},{96,112},{112,128},... | collective-permute-start | bytes 196616 | tf_op jit(solution)/shard_map/while/body/eval_jaxpr/ppermute | solution.py:12
  128.0 10.0 %collective-permute-start.1 = (f32[1,4,4096]{2,1,0:T(4,128)S(1)}, f32[1,4,4096]{2,1,0:T(4,128)S(1)}, u32[]{:S(2)}, u32[]{:S(2)}) collective-permute-start(f32[1,4,4096]{2,1,0:T(4,128)S(1)} %get-tuple-element.435), channel_id=1, source_target_pairs={{0,16},{16,32},{32,48},{48,64},{64,80},{80,96},{96,112},{112,128},... | collective-permute-start | bytes 196616 | tf_op jit(solution)/shard_map/while/body/eval_jaxpr/ppermute | solution.py:12
  129.9 7.6 %collective-permute-start = (s32[1,4]{1,0:T(1,128)S(1)}, s32[1,4]{1,0:T(1,128)S(1)}, u32[]{:S(2)}, u32[]{:S(2)}) collective-permute-start(s32[1,4]{1,0:T(1,128)S(1)} %get-tuple-element.436), channel_id=1, source_target_pairs={{0,16},{16,32},{32,48},{48,64},{64,80},{80,96},{96,112},{112,128},... | collective-permute-start | bytes 56 | tf_op jit(solution)/shard_map/while/body/eval_jaxpr/ppermute | solution.py:12
  145.1 10.0 %collective-permute-start.1 = (f32[1,4,4096]{2,1,0:T(4,128)S(1)}, f32[1,4,4096]{2,1,0:T(4,128)S(1)}, u32[]{:S(2)}, u32[]{:S(2)}) collective-permute-start(f32[1,4,4096]{2,1,0:T(4,128)S(1)} %get-tuple-element.435), channel_id=1, source_target_pairs={{0,16},{16,32},{32,48},{48,64},{64,80},{80,96},{96,112},{112,128},... | collective-permute-start | bytes 196616 | tf_op jit(solution)/shard_map/while/body/eval_jaxpr/ppermute | solution.py:12
  147.0 7.6 %collective-permute-start = (s32[1,4]{1,0:T(1,128)S(1)}, s32[1,4]{1,0:T(1,128)S(1)}, u32[]{:S(2)}, u32[]{:S(2)}) collective-permute-start(s32[1,4]{1,0:T(1,128)S(1)} %get-tuple-element.436), channel_id=1, source_target_pairs={{0,16},{16,32},{32,48},{48,64},{64,80},{80,96},{96,112},{112,128},... | collective-permute-start | bytes 56 | tf_op jit(solution)/shard_map/while/body/eval_jaxpr/ppermute | solution.py:12
  162.2 10.0 %collective-permute-start.1 = (f32[1,4,4096]{2,1,0:T(4,128)S(1)}, f32[1,4,4096]{2,1,0:T(4,128)S(1)}, u32[]{:S(2)}, u32[]{:S(2)}) collective-permute-start(f32[1,4,4096]{2,1,0:T(4,128)S(1)} %get-tuple-element.435), channel_id=1, source_target_pairs={{0,16},{16,32},{32,48},{48,64},{64,80},{80,96},{96,112},{112,128},... | collective-permute-start | bytes 196616 | tf_op jit(solution)/shard_map/while/body/eval_jaxpr/ppermute | solution.py:12
  164.2 7.6 %collective-permute-start = (s32[1,4]{1,0:T(1,128)S(1)}, s32[1,4]{1,0:T(1,128)S(1)}, u32[]{:S(2)}, u32[]{:S(2)}) collective-permute-start(s32[1,4]{1,0:T(1,128)S(1)} %get-tuple-element.436), channel_id=1, source_target_pairs={{0,16},{16,32},{32,48},{48,64},{64,80},{80,96},{96,112},{112,128},... | collective-permute-start | bytes 56 | tf_op jit(solution)/shard_map/while/body/eval_jaxpr/ppermute | solution.py:12
  179.4 10.0 %collective-permute-start.1 = (f32[1,4,4096]{2,1,0:T(4,128)S(1)}, f32[1,4,4096]{2,1,0:T(4,128)S(1)}, u32[]{:S(2)}, u32[]{:S(2)}) collective-permute-start(f32[1,4,4096]{2,1,0:T(4,128)S(1)} %get-tuple-element.435), channel_id=1, source_target_pairs={{0,16},{16,32},{32,48},{48,64},{64,80},{80,96},{96,112},{112,128},... | collective-permute-start | bytes 196616 | tf_op jit(solution)/shard_map/while/body/eval_jaxpr/ppermute | solution.py:12
  181.3 7.6 %collective-permute-start = (s32[1,4]{1,0:T(1,128)S(1)}, s32[1,4]{1,0:T(1,128)S(1)}, u32[]{:S(2)}, u32[]{:S(2)}) collective-permute-start(s32[1,4]{1,0:T(1,128)S(1)} %get-tuple-element.436), channel_id=1, source_target_pairs={{0,16},{16,32},{32,48},{48,64},{64,80},{80,96},{96,112},{112,128},... | collective-permute-start | bytes 56 | tf_op jit(solution)/shard_map/while/body/eval_jaxpr/ppermute | solution.py:12
  196.5 10.0 %collective-permute-start.1 = (f32[1,4,4096]{2,1,0:T(4,128)S(1)}, f32[1,4,4096]{2,1,0:T(4,128)S(1)}, u32[]{:S(2)}, u32[]{:S(2)}) collective-permute-start(f32[1,4,4096]{2,1,0:T(4,128)S(1)} %get-tuple-element.435), channel_id=1, source_target_pairs={{0,16},{16,32},{32,48},{48,64},{64,80},{80,96},{96,112},{112,128},... | collective-permute-start | bytes 196616 | tf_op jit(solution)/shard_map/while/body/eval_jaxpr/ppermute | solution.py:12
  198.4 7.6 %collective-permute-start = (s32[1,4]{1,0:T(1,128)S(1)}, s32[1,4]{1,0:T(1,128)S(1)}, u32[]{:S(2)}, u32[]{:S(2)}) collective-permute-start(s32[1,4]{1,0:T(1,128)S(1)} %get-tuple-element.436), channel_id=1, source_target_pairs={{0,16},{16,32},{32,48},{48,64},{64,80},{80,96},{96,112},{112,128},... | collective-permute-start | bytes 56 | tf_op jit(solution)/shard_map/while/body/eval_jaxpr/ppermute | solution.py:12
  213.6 10.0 %collective-permute-start.1 = (f32[1,4,4096]{2,1,0:T(4,128)S(1)}, f32[1,4,4096]{2,1,0:T(4,128)S(1)}, u32[]{:S(2)}, u32[]{:S(2)}) collective-permute-start(f32[1,4,4096]{2,1,0:T(4,128)S(1)} %get-tuple-element.435), channel_id=1, source_target_pairs={{0,16},{16,32},{32,48},{48,64},{64,80},{80,96},{96,112},{112,128},... | collective-permute-start | bytes 196616 | tf_op jit(solution)/shard_map/while/body/eval_jaxpr/ppermute | solution.py:12
  215.6 7.6 %collective-permute-start = (s32[1,4]{1,0:T(1,128)S(1)}, s32[1,4]{1,0:T(1,128)S(1)}, u32[]{:S(2)}, u32[]{:S(2)}) collective-permute-start(s32[1,4]{1,0:T(1,128)S(1)} %get-tuple-element.436), channel_id=1, source_target_pairs={{0,16},{16,32},{32,48},{48,64},{64,80},{80,96},{96,112},{112,128},... | collective-permute-start | bytes 56 | tf_op jit(solution)/shard_map/while/body/eval_jaxpr/ppermute | solution.py:12
  230.8 10.0 %collective-permute-start.1 = (f32[1,4,4096]{2,1,0:T(4,128)S(1)}, f32[1,4,4096]{2,1,0:T(4,128)S(1)}, u32[]{:S(2)}, u32[]{:S(2)}) collective-permute-start(f32[1,4,4096]{2,1,0:T(4,128)S(1)} %get-tuple-element.435), channel_id=1, source_target_pairs={{0,16},{16,32},{32,48},{48,64},{64,80},{80,96},{96,112},{112,128},... | collective-permute-start | bytes 196616 | tf_op jit(solution)/shard_map/while/body/eval_jaxpr/ppermute | solution.py:12
  232.7 7.6 %collective-permute-start = (s32[1,4]{1,0:T(1,128)S(1)}, s32[1,4]{1,0:T(1,128)S(1)}, u32[]{:S(2)}, u32[]{:S(2)}) collective-permute-start(s32[1,4]{1,0:T(1,128)S(1)} %get-tuple-element.436), channel_id=1, source_target_pairs={{0,16},{16,32},{32,48},{48,64},{64,80},{80,96},{96,112},{112,128},... | collective-permute-start | bytes 56 | tf_op jit(solution)/shard_map/while/body/eval_jaxpr/ppermute | solution.py:12
  247.9 10.3 %collective-permute-start.1 = (f32[1,4,4096]{2,1,0:T(4,128)S(1)}, f32[1,4,4096]{2,1,0:T(4,128)S(1)}, u32[]{:S(2)}, u32[]{:S(2)}) collective-permute-start(f32[1,4,4096]{2,1,0:T(4,128)S(1)} %get-tuple-element.435), channel_id=1, source_target_pairs={{0,16},{16,32},{32,48},{48,64},{64,80},{80,96},{96,112},{112,128},... | collective-permute-start | bytes 196616 | tf_op jit(solution)/shard_map/while/body/eval_jaxpr/ppermute | solution.py:12
  249.8 7.9 %collective-permute-start = (s32[1,4]{1,0:T(1,128)S(1)}, s32[1,4]{1,0:T(1,128)S(1)}, u32[]{:S(2)}, u32[]{:S(2)}) collective-permute-start(s32[1,4]{1,0:T(1,128)S(1)} %get-tuple-element.436), channel_id=1, source_target_pairs={{0,16},{16,32},{32,48},{48,64},{64,80},{80,96},{96,112},{112,128},... | collective-permute-start | bytes 56 | tf_op jit(solution)/shard_map/while/body/eval_jaxpr/ppermute | solution.py:12
  265.3 10.0 %collective-permute-start.1 = (f32[1,4,4096]{2,1,0:T(4,128)S(1)}, f32[1,4,4096]{2,1,0:T(4,128)S(1)}, u32[]{:S(2)}, u32[]{:S(2)}) collective-permute-start(f32[1,4,4096]{2,1,0:T(4,128)S(1)} %get-tuple-element.435), channel_id=1, source_target_pairs={{0,16},{16,32},{32,48},{48,64},{64,80},{80,96},{96,112},{112,128},... | collective-permute-start | bytes 196616 | tf_op jit(solution)/shard_map/while/body/eval_jaxpr/ppermute | solution.py:12
  267.3 7.6 %collective-permute-start = (s32[1,4]{1,0:T(1,128)S(1)}, s32[1,4]{1,0:T(1,128)S(1)}, u32[]{:S(2)}, u32[]{:S(2)}) collective-permute-start(s32[1,4]{1,0:T(1,128)S(1)} %get-tuple-element.436), channel_id=1, source_target_pairs={{0,16},{16,32},{32,48},{48,64},{64,80},{80,96},{96,112},{112,128},... | collective-permute-start | bytes 56 | tf_op jit(solution)/shard_map/while/body/eval_jaxpr/ppermute | solution.py:12
  282.5 10.0 %collective-permute-start.1 = (f32[1,4,4096]{2,1,0:T(4,128)S(1)}, f32[1,4,4096]{2,1,0:T(4,128)S(1)}, u32[]{:S(2)}, u32[]{:S(2)}) collective-permute-start(f32[1,4,4096]{2,1,0:T(4,128)S(1)} %get-tuple-element.435), channel_id=1, source_target_pairs={{0,16},{16,32},{32,48},{48,64},{64,80},{80,96},{96,112},{112,128},... | collective-permute-start | bytes 196616 | tf_op jit(solution)/shard_map/while/body/eval_jaxpr/ppermute | solution.py:12
  284.4 7.6 %collective-permute-start = (s32[1,4]{1,0:T(1,128)S(1)}, s32[1,4]{1,0:T(1,128)S(1)}, u32[]{:S(2)}, u32[]{:S(2)}) collective-permute-start(s32[1,4]{1,0:T(1,128)S(1)} %get-tuple-element.436), channel_id=1, source_target_pairs={{0,16},{16,32},{32,48},{48,64},{64,80},{80,96},{96,112},{112,128},... | collective-permute-start | bytes 56 | tf_op jit(solution)/shard_map/while/body/eval_jaxpr/ppermute | solution.py:12
  299.6 10.0 %collective-permute-start.1 = (f32[1,4,4096]{2,1,0:T(4,128)S(1)}, f32[1,4,4096]{2,1,0:T(4,128)S(1)}, u32[]{:S(2)}, u32[]{:S(2)}) collective-permute-start(f32[1,4,4096]{2,1,0:T(4,128)S(1)} %get-tuple-element.435), channel_id=1, source_target_pairs={{0,16},{16,32},{32,48},{48,64},{64,80},{80,96},{96,112},{112,128},... | collective-permute-start | bytes 196616 | tf_op jit(solution)/shard_map/while/body/eval_jaxpr/ppermute | solution.py:12
  301.5 7.6 %collective-permute-start = (s32[1,4]{1,0:T(1,128)S(1)}, s32[1,4]{1,0:T(1,128)S(1)}, u32[]{:S(2)}, u32[]{:S(2)}) collective-permute-start(s32[1,4]{1,0:T(1,128)S(1)} %get-tuple-element.436), channel_id=1, source_target_pairs={{0,16},{16,32},{32,48},{48,64},{64,80},{80,96},{96,112},{112,128},... | collective-permute-start | bytes 56 | tf_op jit(solution)/shard_map/while/body/eval_jaxpr/ppermute | solution.py:12
  316.7 10.0 %collective-permute-start.1 = (f32[1,4,4096]{2,1,0:T(4,128)S(1)}, f32[1,4,4096]{2,1,0:T(4,128)S(1)}, u32[]{:S(2)}, u32[]{:S(2)}) collective-permute-start(f32[1,4,4096]{2,1,0:T(4,128)S(1)} %get-tuple-element.435), channel_id=1, source_target_pairs={{0,16},{16,32},{32,48},{48,64},{64,80},{80,96},{96,112},{112,128},... | collective-permute-start | bytes 196616 | tf_op jit(solution)/shard_map/while/body/eval_jaxpr/ppermute | solution.py:12
  333.9 10.0 %collective-permute-start.1 = (f32[1,4,4096]{2,1,0:T(4,128)S(1)}, f32[1,4,4096]{2,1,0:T(4,128)S(1)}, u32[]{:S(2)}, u32[]{:S(2)}) collective-permute-start(f32[1,4,4096]{2,1,0:T(4,128)S(1)} %get-tuple-element.435), channel_id=1, source_target_pairs={{0,16},{16,32},{32,48},{48,64},{64,80},{80,96},{96,112},{112,128},... | collective-permute-start | bytes 196616 | tf_op jit(solution)/shard_map/while/body/eval_jaxpr/ppermute | solution.py:12
  351.0 10.0 %collective-permute-start.1 = (f32[1,4,4096]{2,1,0:T(4,128)S(1)}, f32[1,4,4096]{2,1,0:T(4,128)S(1)}, u32[]{:S(2)}, u32[]{:S(2)}) collective-permute-start(f32[1,4,4096]{2,1,0:T(4,128)S(1)} %get-tuple-element.435), channel_id=1, source_target_pairs={{0,16},{16,32},{32,48},{48,64},{64,80},{80,96},{96,112},{112,128},... | collective-permute-start | bytes 196616 | tf_op jit(solution)/shard_map/while/body/eval_jaxpr/ppermute | solution.py:12
  368.1 10.0 %collective-permute-start.1 = (f32[1,4,4096]{2,1,0:T(4,128)S(1)}, f32[1,4,4096]{2,1,0:T(4,128)S(1)}, u32[]{:S(2)}, u32[]{:S(2)}) collective-permute-start(f32[1,4,4096]{2,1,0:T(4,128)S(1)} %get-tuple-element.435), channel_id=1, source_target_pairs={{0,16},{16,32},{32,48},{48,64},{64,80},{80,96},{96,112},{112,128},... | collective-permute-start | bytes 196616 | tf_op jit(solution)/shard_map/while/body/eval_jaxpr/ppermute | solution.py:12
  385.3 10.0 %collective-permute-start.1 = (f32[1,4,4096]{2,1,0:T(4,128)S(1)}, f32[1,4,4096]{2,1,0:T(4,128)S(1)}, u32[]{:S(2)}, u32[]{:S(2)}) collective-permute-start(f32[1,4,4096]{2,1,0:T(4,128)S(1)} %get-tuple-element.435), channel_id=1, source_target_pairs={{0,16},{16,32},{32,48},{48,64},{64,80},{80,96},{96,112},{112,128},... | collective-permute-start | bytes 196616 | tf_op jit(solution)/shard_map/while/body/eval_jaxpr/ppermute | solution.py:12
  402.4 10.0 %collective-permute-start.1 = (f32[1,4,4096]{2,1,0:T(4,128)S(1)}, f32[1,4,4096]{2,1,0:T(4,128)S(1)}, u32[]{:S(2)}, u32[]{:S(2)}) collective-permute-start(f32[1,4,4096]{2,1,0:T(4,128)S(1)} %get-tuple-element.435), channel_id=1, source_target_pairs={{0,16},{16,32},{32,48},{48,64},{64,80},{80,96},{96,112},{112,128},... | collective-permute-start | bytes 196616 | tf_op jit(solution)/shard_map/while/body/eval_jaxpr/ppermute | solution.py:12
  419.5 10.0 %collective-permute-start.1 = (f32[1,4,4096]{2,1,0:T(4,128)S(1)}, f32[1,4,4096]{2,1,0:T(4,128)S(1)}, u32[]{:S(2)}, u32[]{:S(2)}) collective-permute-start(f32[1,4,4096]{2,1,0:T(4,128)S(1)} %get-tuple-element.435), channel_id=1, source_target_pairs={{0,16},{16,32},{32,48},{48,64},{64,80},{80,96},{96,112},{112,128},... | collective-permute-start | bytes 196616 | tf_op jit(solution)/shard_map/while/body/eval_jaxpr/ppermute | solution.py:12
  436.7 10.0 %collective-permute-start.1 = (f32[1,4,4096]{2,1,0:T(4,128)S(1)}, f32[1,4,4096]{2,1,0:T(4,128)S(1)}, u32[]{:S(2)}, u32[]{:S(2)}) collective-permute-start(f32[1,4,4096]{2,1,0:T(4,128)S(1)} %get-tuple-element.435), channel_id=1, source_target_pairs={{0,16},{16,32},{32,48},{48,64},{64,80},{80,96},{96,112},{112,128},... | collective-permute-start | bytes 196616 | tf_op jit(solution)/shard_map/while/body/eval_jaxpr/ppermute | solution.py:12
  453.8 10.0 %collective-permute-start.1 = (f32[1,4,4096]{2,1,0:T(4,128)S(1)}, f32[1,4,4096]{2,1,0:T(4,128)S(1)}, u32[]{:S(2)}, u32[]{:S(2)}) collective-permute-start(f32[1,4,4096]{2,1,0:T(4,128)S(1)} %get-tuple-element.435), channel_id=1, source_target_pairs={{0,16},{16,32},{32,48},{48,64},{64,80},{80,96},{96,112},{112,128},... | collective-permute-start | bytes 196616 | tf_op jit(solution)/shard_map/while/body/eval_jaxpr/ppermute | solution.py:12
  470.9 10.0 %collective-permute-start.1 = (f32[1,4,4096]{2,1,0:T(4,128)S(1)}, f32[1,4,4096]{2,1,0:T(4,128)S(1)}, u32[]{:S(2)}, u32[]{:S(2)}) collective-permute-start(f32[1,4,4096]{2,1,0:T(4,128)S(1)} %get-tuple-element.435), channel_id=1, source_target_pairs={{0,16},{16,32},{32,48},{48,64},{64,80},{80,96},{96,112},{112,128},... | collective-permute-start | bytes 196616 | tf_op jit(solution)/shard_map/while/body/eval_jaxpr/ppermute | solution.py:12
  488.1 10.0 %collective-permute-start.1 = (f32[1,4,4096]{2,1,0:T(4,128)S(1)}, f32[1,4,4096]{2,1,0:T(4,128)S(1)}, u32[]{:S(2)}, u32[]{:S(2)}) collective-permute-start(f32[1,4,4096]{2,1,0:T(4,128)S(1)} %get-tuple-element.435), channel_id=1, source_target_pairs={{0,16},{16,32},{32,48},{48,64},{64,80},{80,96},{96,112},{112,128},... | collective-permute-start | bytes 196616 | tf_op jit(solution)/shard_map/while/body/eval_jaxpr/ppermute | solution.py:12
  505.2 10.0 %collective-permute-start.1 = (f32[1,4,4096]{2,1,0:T(4,128)S(1)}, f32[1,4,4096]{2,1,0:T(4,128)S(1)}, u32[]{:S(2)}, u32[]{:S(2)}) collective-permute-start(f32[1,4,4096]{2,1,0:T(4,128)S(1)} %get-tuple-element.435), channel_id=1, source_target_pairs={{0,16},{16,32},{32,48},{48,64},{64,80},{80,96},{96,112},{112,128},... | collective-permute-start | bytes 196616 | tf_op jit(solution)/shard_map/while/body/eval_jaxpr/ppermute | solution.py:12
  507.1 7.6 %collective-permute-start = (s32[1,4]{1,0:T(1,128)S(1)}, s32[1,4]{1,0:T(1,128)S(1)}, u32[]{:S(2)}, u32[]{:S(2)}) collective-permute-start(s32[1,4]{1,0:T(1,128)S(1)} %get-tuple-element.436), channel_id=1, source_target_pairs={{0,16},{16,32},{32,48},{48,64},{64,80},{80,96},{96,112},{112,128},... | collective-permute-start | bytes 56 | tf_op jit(solution)/shard_map/while/body/eval_jaxpr/ppermute | solution.py:12
  522.3 10.3 %collective-permute-start.1 = (f32[1,4,4096]{2,1,0:T(4,128)S(1)}, f32[1,4,4096]{2,1,0:T(4,128)S(1)}, u32[]{:S(2)}, u32[]{:S(2)}) collective-permute-start(f32[1,4,4096]{2,1,0:T(4,128)S(1)} %get-tuple-element.435), channel_id=1, source_target_pairs={{0,16},{16,32},{32,48},{48,64},{64,80},{80,96},{96,112},{112,128},... | collective-permute-start | bytes 196616 | tf_op jit(solution)/shard_map/while/body/eval_jaxpr/ppermute | solution.py:12
  524.3 7.9 %collective-permute-start = (s32[1,4]{1,0:T(1,128)S(1)}, s32[1,4]{1,0:T(1,128)S(1)}, u32[]{:S(2)}, u32[]{:S(2)}) collective-permute-start(s32[1,4]{1,0:T(1,128)S(1)} %get-tuple-element.436), channel_id=1, source_target_pairs={{0,16},{16,32},{32,48},{48,64},{64,80},{80,96},{96,112},{112,128},... | collective-permute-start | bytes 56 | tf_op jit(solution)/shard_map/while/body/eval_jaxpr/ppermute | solution.py:12
  539.8 10.0 %collective-permute-start.1 = (f32[1,4,4096]{2,1,0:T(4,128)S(1)}, f32[1,4,4096]{2,1,0:T(4,128)S(1)}, u32[]{:S(2)}, u32[]{:S(2)}) collective-permute-start(f32[1,4,4096]{2,1,0:T(4,128)S(1)} %get-tuple-element.435), channel_id=1, source_target_pairs={{0,16},{16,32},{32,48},{48,64},{64,80},{80,96},{96,112},{112,128},... | collective-permute-start | bytes 196616 | tf_op jit(solution)/shard_map/while/body/eval_jaxpr/ppermute | solution.py:12
  (19 other events, 223.3 us)
Sparse Core Ops, SparseCore 0:
  563.6 97.0 reduce-scatter.1
where the time goes:
time: 675 us; the launch traced here: 670 us
  matrix products  212 us (31%)
  waiting for transfers between devices  202 us (30%)
  starting transfers between devices  124 us (18%)
  local copies, waits for them, and re-layouts  80.1 us (12%)
  other arithmetic  34.2 us (5%)
  between operations  13.5 us (2%)
    dot_general x32, matrix products, deposit(): jnp.dot(landing.T, flat_products, precision=lax.Precision.HIGHEST, prefer...  188 us
    ppermute x62, starting transfers between devices, shifted(): lax.ppermute(value, axis, [(i, (i + by) % devices) for i in range(devices)])  124 us
    ppermute x62, waiting for transfers between devices, shifted(): lax.ppermute(value, axis, [(i, (i + by) % devices) for i in range(devices)])  106 us
    reduce_scatter x1, waiting for transfers between devices, body(): summed = lax.psum_scatter(totals, 'layer', scatter_dimension=1, tiled=True)  96.6 us
    dot_general x32, matrix products, deposit(): jnp.einsum('rcxy,rsyz->rcsxz', left_blocks, right_blocks, precision=lax.P...  24.6 us
    gather x32, local copies, waits for them, and re-layouts, deposit(): left_flat[row_index * per_row + slot_pick]  18.7 us
    gather x32, local copies, waits for them, and re-layouts, deposit(): wanted = c_cols[row_index]  18.4 us
  transfers between devices with their start and end apart: 63, of which 32 were waited for; matrix products, arithmetic and copies ran while one was open for 12% of the time, Pallas kernels for 0%

commit v1 on v0

v1 whole, which is shorter than its diff:
```python
import functools

import jax
import jax.numpy as jnp
from jax import lax
from jax.experimental import pallas as pl
from jax.experimental.pallas import tpu as pltpu
from jax.sharding import PartitionSpec as P

NX, NY, NZ = 4, 8, 8
CAP = 6
MESH = pl.DeviceIdType.MESH
F32, BF16, I32 = jnp.float32, jnp.bfloat16, jnp.int32
EXACT = lax.Precision.HIGHEST


def kernel(
    a_ref, acol_ref, b_ref, bcol_ref, ccol_ref, out_ref,
    g0, g1, ap, prod, tab, tab_s, off, off_s, core_out, core_in, z_in,
    loc_sem, ag_send, ag_recv, core_send, core_recv, z_send, z_recv,
):
    rows, per_row = 16, 6
    n_inner = NX * NY
    per_k = 4 * CAP
    zero_block = n_inner * per_k
    me, lay = lax.axis_index("blk"), lax.axis_index("layer")
    x, y = me // NY, me % NY
    z, c = lay // 2, lay % 2

    def blk_of(dx, dy):
        return (x + dx + NX) % NX * NY + (y + dy + NY) % NY

    def layer_of(dz):
        return (z + dz + NZ) % NZ * 2 + c

    sibling = z * 2 + 1 - c
    x_step = {0: (1, 0), 1: (-1, 0), 2: (0, 1), 3: (0, -1)}

    barrier = pltpu.get_barrier_semaphore()
    for d in range(4):
        pl.semaphore_signal(barrier, inc=1, device_id=(blk_of(*x_step[d]), lay), device_id_type=MESH)
    for other in (sibling, layer_of(1), layer_of(-1)):
        pl.semaphore_signal(barrier, inc=1, device_id=(me, other), device_id_type=MESH)

    lane = lax.broadcasted_iota(I32, (32, 128), 1)
    low = lane < 64

    for pair in range(2):
        first = b_ref[pl.ds(2 * pair, 32, stride=4), :]
        second = b_ref[pl.ds(2 * pair + 1, 32, stride=4), :]
        even = jnp.where(low, first, pltpu.roll(second, 64, 1))
        odd = jnp.where(low, pltpu.roll(first, 64, 1), second)
        g = g0 if pair == 0 else g1
        g[me, pl.ds(0, 32, stride=2), :] = even
        g[me, pl.ds(1, 32, stride=2), :] = odd
    sub8 = lax.broadcasted_iota(I32, (8, 128), 0)
    meta = jnp.full((8, 128), -1, I32)
    for s in range(4):
        meta = jnp.where(sub8 == s, bcol_ref[0, s], meta)
    g0[me, 64:72, :] = meta.astype(F32)

    pl.semaphore_wait(barrier, 7)

    def ag_copy(half, k, d):
        buf = g0 if half == 0 else g1
        return pltpu.make_async_remote_copy(
            src_ref=buf.at[k], dst_ref=buf.at[k],
            send_sem=ag_send.at[half, d, k], recv_sem=ag_recv.at[half, k],
            device_id=(blk_of(*x_step[d]), lay), device_id_type=MESH,
        )

    def act(half, k, d, what):
        copy = ag_copy(half, k, d)
        if what == "start":
            copy.start()
        else:
            copy.wait_send()

    def y_sends(half, dx, dy, what):
        k = blk_of(dx, dy)
        even = (x + dx + NX) % 2 == 0
        if -2 <= dy <= 0:
            act(half, k, 2, what)
        if 0 <= dy <= 2:
            act(half, k, 3, what)
        if dy == -3:
            pl.when(even)(lambda: act(half, k, 2, what))
        if dy == 3:
            pl.when(jnp.logical_not(even))(lambda: act(half, k, 3, what))

    def x_sends(half, dx, dy, what):
        k = blk_of(dx, dy)
        even = (y + dy + NY) % 2 == 0
        if dx == 0:
            act(half, k, 0, what)
            act(half, k, 1, what)
        if dx == -1:
            pl.when(even)(lambda: act(half, k, 0, what))
        if dx == 1:
            pl.when(jnp.logical_not(even))(lambda: act(half, k, 1, what))

    def arrive(half, dx, dy):
        ag_copy(half, blk_of(dx, dy), 0).wait_recv()

    x_sends(0, 0, 0, "start")
    y_sends(1, 0, 0, "start")
    x_sends(1, 0, 0, "start")
    y_sends(0, 0, 0, "start")

    tile = (lax.broadcasted_iota(I32, (rows, 128), 1) % rows == lax.broadcasted_iota(I32, (rows, 128), 0)).astype(F32)
    spread = jnp.dot(acol_ref[...].astype(F32), tile, preferred_element_type=F32, precision=EXACT)
    lane6 = lax.broadcasted_iota(I32, (per_row, 128), 1)
    mine6 = lane6 // rows == lax.broadcasted_iota(I32, (per_row, 128), 0)
    a_lane = jnp.sum(jnp.where(mine6, spread, 0.0), axis=0, keepdims=True)
    lane1 = lax.broadcasted_iota(I32, (1, 128), 1)
    a_lane = jnp.where(lane1 < rows * per_row, a_lane, -1.0)
    inner = lax.broadcasted_iota(I32, (n_inner, 128), 0).astype(F32)
    onehot = (inner == a_lane).astype(F32)
    before = (lax.broadcasted_iota(I32, (128, 128), 0) < lax.broadcasted_iota(I32, (128, 128), 1)).astype(F32)
    count = jnp.dot(onehot, before, preferred_element_type=F32, precision=EXACT)
    rank = jnp.sum(onehot * count, axis=0, keepdims=True)
    table = jnp.zeros((n_inner, 128), F32)
    lane_f = lane.astype(F32)
    for r in range(CAP):
        hit = jnp.where(count == float(r), onehot, 0.0)
        table = jnp.where(lane == r, jnp.sum(hit * lane_f, axis=1, keepdims=True), table)
    tab[...] = jnp.clip(table.astype(I32), 0, rows * per_row - 1)
    tab_copy = pltpu.make_async_copy(tab, tab_s, loc_sem.at[0])
    tab_copy.start()

    def prepare(n, carry):
        a, i = n // rows, n % rows
        block = a_ref[a, i // 8, pl.ds(i % 8, 32, stride=8), :]
        high = block.astype(BF16).astype(F32)
        rest = block - high
        ap[n, 0:32, :] = jnp.where(low, high, pltpu.roll(rest, 64, 1)).astype(BF16)
        ap[n, 32:64, :] = jnp.where(low, pltpu.roll(high, 64, 1), rest).astype(BF16)
        return carry

    lax.fori_loop(0, rows * per_row, prepare, 0)
    prod[zero_block] = jnp.zeros((32, 128), F32)
    tab_copy.wait()

    def products(k):
        right = jnp.concatenate([g0[k, 0:64, :], g1[k]], axis=1)
        high = right.astype(BF16)
        rest = (right - high.astype(F32)).astype(BF16)
        weights = jnp.concatenate([high, high, rest, rest], axis=0)
        left = jnp.concatenate([ap[tab_s[k, r]] for r in range(CAP)], axis=0)
        left = jnp.concatenate([left, left], axis=1)
        both = jnp.dot(left, weights, preferred_element_type=F32)
        for r in range(CAP):
            for pair in range(2):
                even = both[r * 64:r * 64 + 32, pair * 128:pair * 128 + 128]
                odd = both[r * 64 + 32:r * 64 + 64, pair * 128:pair * 128 + 128]
                prod[k * per_k + 2 * pair * CAP + r] = jnp.where(low, even, pltpu.roll(odd, 64, 1))
                prod[k * per_k + (2 * pair + 1) * CAP + r] = jnp.where(low, pltpu.roll(even, 64, 1), odd)

    def stage_dys(h):
        return [0] if h == 0 else ([4] if h == 4 else [-h, h])

    def stage_products(h):
        dys = stage_dys(h)

        def one(u, carry):
            dy = h if len(dys) == 1 else h * (2 * (u // NX) - 1)
            products((x + u) % NX * NY + (y + dy + NY) % NY)
            return carry

        lax.fori_loop(0, NX * len(dys), one, 0)

    for h in range(7):
        if h == 0:
            for dx in (-1, 1, 2):
                arrive(0, dx, 0)
                x_sends(0, dx, 0, "start")
                y_sends(0, dx, 0, "start")
        elif h <= 4:
            for dy in stage_dys(h):
                arrive(1, 0, dy)
                y_sends(1, 0, dy, "start")
                x_sends(1, 0, dy, "start")
                for dx in (0, -1, 1, 2):
                    arrive(0, dx, dy)
                    y_sends(0, dx, dy, "start")
        if 1 <= h <= 5:
            for dy in stage_dys(h - 1):
                for dx in (-1, 1):
                    arrive(1, dx, dy)
                    x_sends(1, dx, dy, "start")
        if h >= 2:
            for dy in stage_dys(h - 2):
                arrive(1, 2, dy)
            stage_products(h - 2)

    target = lax.dot_general(ccol_ref[...].astype(F32), tile, (((0,), (0,)), ((), ())), preferred_element_type=F32, precision=EXACT)

    def pick(k, cols):
        return jnp.where(a_lane == k.astype(F32), g0[k, 64:72, :], cols)

    cols = lax.fori_loop(0, n_inner, pick, jnp.full((8, 128), -1.0, F32))
    base = a_lane * float(per_k) + rank
    where_from = jnp.full((rows, 128), float(zero_block), F32)
    for s in range(4):
        where_from = jnp.where(target == cols[s:s + 1, :], base + float(CAP * s), where_from)
    off[...] = jnp.clip(where_from.astype(I32), 0, zero_block)
    off_copy = pltpu.make_async_copy(off, off_s, loc_sem.at[1])
    off_copy.start()
    off_copy.wait()

    def landed(m, i):
        total = prod[off_s[m, i]]
        for a in range(1, per_row):
            total = total + prod[off_s[m, a * rows + i]]
        return total

    def core_copy(part, delta):
        slot = part * NZ + delta % NZ
        return pltpu.make_async_remote_copy(
            src_ref=core_out.at[slot], dst_ref=core_in.at[slot],
            send_sem=core_send.at[slot], recv_sem=core_recv.at[slot],
            device_id=(me, sibling), device_id_type=MESH,
        )

    def give(part, delta):
        slot = part * NZ + delta % NZ
        m = (z + delta + NZ) % NZ * 2 + 1 - c

        def one(i, carry):
            core_out[slot, i] = landed(m, part * 8 + i)
            return carry

        lax.fori_loop(0, 8, one, 0)
        core_copy(part, delta).start()

    def z_copy(way, part, t):
        slot = (way * 2 + part) * 4 + t - 1
        source = core_in.at[part * NZ + z_delta(way, part, t) % NZ]
        return pltpu.make_async_remote_copy(
            src_ref=source, dst_ref=z_in.at[slot],
            send_sem=z_send.at[slot], recv_sem=z_recv.at[slot],
            device_id=(me, layer_of(1 - 2 * way)), device_id_type=MESH,
        )

    def z_steps(way, part):
        return 4 if way == part else 3

    def z_delta(way, part, t):
        return (z_steps(way, part) + 1 - t) * (1 - 2 * way)

    def pass_on(way, part, t):
        delta = z_delta(way, part, t)
        slot = part * NZ + delta % NZ
        m = (z + delta + NZ) % NZ * 2 + c
        core_copy(part, delta).wait_recv()
        if t > 1:
            z_copy(way, part, t - 1).wait_recv()

        def one(i, carry):
            total = landed(m, part * 8 + i) + core_in[slot, i]
            if t > 1:
                total = total + z_in[(way * 2 + part) * 4 + t - 2, i]
            core_in[slot, i] = total
            return carry

        lax.fori_loop(0, 8, one, 0)
        z_copy(way, part, t).start()

    def pieces(t):
        return [(way, part) for way, part in ((0, 0), (1, 1), (0, 1), (1, 0)) if t <= z_steps(way, part)]

    def give_all(t):
        if t <= 4:
            for way, part in pieces(t):
                give(part, z_delta(way, part, t))
        else:
            give(0, 0)
            give(1, 0)

    give_all(1)
    for t in range(1, 5):
        give_all(t + 1)
        for way, part in pieces(t):
            pass_on(way, part, t)

    for part in range(2):
        core_copy(part, 0).wait_recv()
        for way in range(2):
            z_copy(way, part, z_steps(way, part)).wait_recv()

        def one(i, carry):
            total = landed(z * 2 + c, part * 8 + i) + core_in[part * NZ, i]
            for way in range(2):
                total = total + z_in[(way * 2 + part) * 4 + z_steps(way, part) - 1, i]
            out_ref[part * 8 + i] = total
            return carry

        lax.fori_loop(0, 8, one, 0)

    for h in range(5):
        for dy in stage_dys(h):
            for dx in (0, -1, 1, 2):
                y_sends(0, dx, dy, "wait")
                x_sends(1, dx, dy, "wait")
            y_sends(1, 0, dy, "wait")
    for dx in (0, -1, 1):
        x_sends(0, dx, 0, "wait")
    for part in range(2):
        for delta in range(NZ):
            core_copy(part, delta).wait_send()
    for t in range(1, 5):
        for way, part in pieces(t):
            z_copy(way, part, t).wait_send()


def body(a_vals, a_cols, b_vals, b_cols, c_cols, c_keep, c_vals):
    n_inner = NX * NY
    a = jnp.transpose(a_vals[0], (1, 0, 2)).reshape(6, 2, 8, 32, 128)
    a = jnp.transpose(a, (0, 1, 3, 2, 4)).reshape(6, 2, 256, 128)
    b = jnp.transpose(b_vals[0].reshape(4, 32, 128), (1, 0, 2)).reshape(128, 128)
    vmem = pl.BlockSpec(memory_space=pltpu.VMEM)
    smem = pl.BlockSpec(memory_space=pltpu.SMEM)
    dma = pltpu.SemaphoreType.DMA
    summed = pl.pallas_call(
        kernel,
        out_shape=jax.ShapeDtypeStruct((16, 32, 128), F32),
        in_specs=[vmem, vmem, vmem, smem, vmem],
        out_specs=vmem,
        scratch_shapes=[
            pltpu.VMEM((n_inner, 72, 128), F32),
            pltpu.VMEM((n_inner, 64, 128), F32),
            pltpu.VMEM((96, 64, 128), BF16),
            pltpu.VMEM((n_inner * 4 * CAP + 1, 32, 128), F32),
            pltpu.VMEM((n_inner, 128), I32),
            pltpu.SMEM((n_inner, 128), I32),
            pltpu.VMEM((16, 128), I32),
            pltpu.SMEM((16, 128), I32),
            pltpu.VMEM((16, 8, 32, 128), F32),
            pltpu.VMEM((16, 8, 32, 128), F32),
            pltpu.VMEM((16, 8, 32, 128), F32),
            dma((2,)),
            dma((2, 4, n_inner)),
            dma((2, n_inner)),
            dma((16,)),
            dma((16,)),
            dma((16,)),
            dma((16,)),
        ],
        compiler_params=pltpu.CompilerParams(
            collective_id=0, has_side_effects=True, vmem_limit_bytes=48 << 20
        ),
        cost_estimate=pl.CostEstimate(flops=1 << 31, bytes_accessed=8 << 20, transcendentals=0),
    )(a, a_cols[0].T, b, b_cols, c_cols)
    keep = c_keep.astype(F32)[:, :, None]
    return keep * (1.5 * c_vals - 0.5 * summed.reshape(16, 1, 4096))


def solution(mesh):
    in_specs = (
        P("layer", "blk", None, None),
        P("layer", "blk", None),
        P(("blk", "layer"), None, None),
        P(("blk", "layer"), None),
        P("blk", None),
        P("blk", "layer"),
        P("blk", "layer", None),
    )
    out_specs = P("blk", "layer", None)
    return jax.shard_map(body, mesh=mesh, in_specs=in_specs, out_specs=out_specs, check_vma=False)
```

time: 675 us -> 85.4 us (0.13)
  matrix products: 212 us -> 0 us
  waiting for transfers between devices: 202 us -> 0 us
  starting transfers between devices: 124 us -> 0 us
  Pallas kernels: 0 us -> 78.9 us
  local copies, waits for them, and re-layouts: 80.1 us -> 4.29 us
  other arithmetic: 34.2 us -> 1.74 us
  between operations: 13.5 us -> 0.03 us
    dot_general x64 -> x0, matrix products: 212 us -> none  [the longest x32 188 us: deposit(): jnp.dot(landing.T, flat_products, precision=lax.Precision.HIGHEST, prefer...]
    ppermute x62 -> x0, starting transfers between devices: 124 us -> none  [shifted(): lax.ppermute(value, axis, [(i, (i + by) % devices) for i in range(devices)])]
    ppermute x62 -> x0, waiting for transfers between devices: 106 us -> none  [shifted(): lax.ppermute(value, axis, [(i, (i + by) % devices) for i in range(devices)])]
    reduce_scatter x1 -> x0, waiting for transfers between devices: 96.6 us -> none  [body(): summed = lax.psum_scatter(totals, 'layer', scatter_dimension=1, tiled=True)]
    pallas_call x0 -> x1, Pallas kernels: none -> 78.9 us  [body(): pl.pallas_call(kernel, out_shape=jax.ShapeDtypeStruct((16, 32, 128), F32)...]
    gather x64 -> x0, local copies, waits for them, and re-layouts: 37.2 us -> none  [the longest x32 18.7 us: deposit(): left_flat[row_index * per_row + slot_pick]]
    reduce_sum x64 -> x0, other arithmetic: 11.5 us -> none  [the longest x32 10.1 us: deposit(): slot_pick = jnp.sum(jnp.where(chosen, slot_index[:, :, None], 0), axis=1)]
    reshape x32 -> x0, local copies, waits for them, and re-layouts: 9.18 us -> none  [deposit(): flat_products = products.reshape(count * capacity * per_brow, block_size)]
  transfers between devices with their start and end apart: 63 -> 0, of which waited for: 32 -> 0; matrix products, arithmetic and copies ran while one was open for 12% -> 0% of each run, Pallas kernels for 0% -> 0%
where the time goes in v1:
time: 85.4 us; the launch traced here: 84.9 us
  Pallas kernels  78.9 us (92%)
  local copies, waits for them, and re-layouts  4.29 us (5%)
  other arithmetic  1.74 us (2%)
    pallas_call x1, Pallas kernels, body(): pl.pallas_call(kernel, out_shape=jax.ShapeDtypeStruct((16, 32, 128), F32)...  78.9 us
    unnamed x11, local copies, waits for them, and re-layouts  4.29 us
    mul x3, other arithmetic, body(): return keep * (1.5 * c_vals - 0.5 * summed.reshape(16, 1, 4096))  1.74 us

profile of v1, /device:TPU:1, one launch (start us, length us, event | category | flops | bytes accessed | tf_op | source)
XLA Modules:
  0.0 84.9 jit_solution(17044289227364778769)
XLA Ops:
  0.0 0.7 convert_bitcast_fusion
  0.7 0.7 copy.12
  1.3 0.0 copy-start
  1.3 1.4 %copy-done = f32[1,16,6,4096]{3,1,2,0:T(8,128)S(1)} copy-done((f32[1,16,6,4096]{3,1,2,0:T(8,128)S(1)}, f32[1,16,6,4096]{3,1,2,0:T(8,128)}, u32[]{:S(2)}) %copy-start) | copy-done | bytes 1572888
  2.8 0.0 copy-start.1
  2.8 0.8 copy-done.1
  3.6 0.0 copy-start.2
  3.6 0.7 copy-done.2
  4.3 0.0 copy-start.3
  4.3 0.7 copy-done.3
  4.9 0.0 copy-start.4
  4.9 78.9 %shard_map.73 = f32[16,32,128]{2,1,0:T(8,128)S(1)} custom-call(f32[6,2,256,128]{3,2,1,0:T(8,128)S(1)} %bitcast.23, s32[6,16]{1,0:T(8,128)S(1)} %bitcast.22, f32[128,128]{1,0:T(8,128)S(1)} %bitcast.24, s32[1,4]{1,0:T(1,128)S(1)} %copy-done.3, s32[16,16]{1,0:T(8,128)S(1)} %copy-done.2), custom_call_target="tpu_custom_call" | custom-call | flops 2147483648 | bytes 8388608 | tf_op jit(solution)/shard_map/pallas_call | solution.py:324
  83.9 0.0 copy-done.4
  83.9 1.1 %subtract_multiply_fusion = f32[16,1,4096]{2,1,0:T(1,128)} fusion(f32[16,1,4096]{2,1,0:T(1,128)S(1)} %bitcast.25, f32[16,1,4096]{2,1,0:T(1,128)S(1)} %copy-done.4, f32[16]{0:T(128)S(1)} %convert_bitcast_fusion), kind=kLoop, calls=%fused_computation | loop fusion | flops 196608 | bytes 786496 | tf_op jit(solution)/shard_map/mul | solution.py:355
  (1 shorter events, 0.0 us)
Async XLA Ops:
  1.3 1.4 %copy-start = (f32[1,16,6,4096]{3,1,2,0:T(8,128)S(1)}, f32[1,16,6,4096]{3,1,2,0:T(8,128)}, u32[]{:S(2)}) copy-start(f32[1,16,6,4096]{3,1,2,0:T(8,128)} %param.7) | copy-start | bytes 4718596
  2.8 0.8 copy-start.1
  3.6 0.7 copy-start.2
  4.3 0.7 copy-start.3
  4.9 78.9 %copy-start.4 = (f32[16,1,4096]{2,1,0:T(1,128)S(1)}, f32[16,1,4096]{2,1,0:T(1,128)}, u32[]{:S(2)}) copy-start(f32[16,1,4096]{2,1,0:T(1,128)} %param.13) | copy-start | bytes 786436

commit v2 on v1

v2 whole, which is shorter than its diff:
```python
import jax
import jax.numpy as jnp
from jax import lax
from jax.experimental import pallas as pl
from jax.experimental.pallas import tpu as pltpu
from jax.sharding import PartitionSpec as P

NX, NY, NZ = 4, 8, 8
CAP = 6
MESH = pl.DeviceIdType.MESH
F32, BF16, I32 = jnp.float32, jnp.bfloat16, jnp.int32
EXACT = lax.Precision.HIGHEST


def kernel(
    a_hbm, acol_hbm, b_hbm, bcol_hbm, ccol_hbm, keep_hbm, cval_hbm, out_ref,
    a_ref, acol_ref, b_ref, bcol_ref, ccol_ref, keep_ref, cval_ref,
    g0, g1, ap, prod, tab, tab_s, off, off_s, core_out, core_in, z_in,
    loc_sem, ag_send, ag_recv, core_send, core_recv, z_send, z_recv,
):
    rows, per_row = 16, 6
    n_inner = NX * NY
    per_k = 4 * CAP
    zero_block = n_inner * per_k
    me, lay = lax.axis_index("blk"), lax.axis_index("layer")
    x, y = me // NY, me % NY
    z, c = lay // 2, lay % 2
    sibling = z * 2 + 1 - c

    def blk_of(dx, dy):
        return (x + dx + NX) % NX * NY + (y + dy + NY) % NY

    def layer_of(dz):
        return (z + dz + NZ) % NZ * 2 + c

    loads = [
        pltpu.make_async_copy(src, dst, loc_sem.at[n])
        for n, (src, dst) in enumerate((
            (b_hbm, b_ref), (bcol_hbm, bcol_ref), (acol_hbm, acol_ref), (ccol_hbm, ccol_ref),
            (keep_hbm, keep_ref), (a_hbm, a_ref), (cval_hbm, cval_ref),
        ))
    ]
    for load in loads:
        load.start()

    steps = ((1, 0), (-1, 0), (0, 1), (0, -1))
    barrier = pltpu.get_barrier_semaphore()
    for step in steps:
        pl.semaphore_signal(barrier, inc=1, device_id=(blk_of(*step), lay), device_id_type=MESH)
    for other in (sibling, layer_of(1), layer_of(-1)):
        pl.semaphore_signal(barrier, inc=1, device_id=(me, other), device_id_type=MESH)

    lane = lax.broadcasted_iota(I32, (32, 128), 1)
    low = lane < 64

    loads[0].wait()
    for pair in range(2):
        first = b_ref[pl.ds(2 * pair, 32, stride=4), :]
        second = b_ref[pl.ds(2 * pair + 1, 32, stride=4), :]
        even = jnp.where(low, first, pltpu.roll(second, 64, 1))
        odd = jnp.where(low, pltpu.roll(first, 64, 1), second)
        g = g0 if pair == 0 else g1
        g[me, pl.ds(0, 32, stride=2), :] = even
        g[me, pl.ds(1, 32, stride=2), :] = odd
    loads[1].wait()
    sub8 = lax.broadcasted_iota(I32, (8, 128), 0)
    meta = jnp.full((8, 128), -1, I32)
    for s in range(4):
        meta = jnp.where(sub8 == s, bcol_ref[0, s], meta)
    g0[me, 64:72, :] = meta.astype(F32)

    pl.semaphore_wait(barrier, 7)

    def ag_copy(half, k, d):
        buf = g0 if half == 0 else g1
        return pltpu.make_async_remote_copy(
            src_ref=buf.at[k], dst_ref=buf.at[k],
            send_sem=ag_send.at[half, d, k], recv_sem=ag_recv.at[half, k],
            device_id=(blk_of(*steps[d]), lay), device_id_type=MESH,
        )

    def act(half, k, d, start):
        if start:
            ag_copy(half, k, d).start()
        else:
            ag_copy(half, k, d).wait_send()

    def arrive(half, dx, dy):
        ag_copy(half, blk_of(dx, dy), 0).wait_recv()

    def send_all(half, k, ds, start):
        for d in ds:
            act(half, k, d, start)

    def y_on(half, dx, h, side, start):
        goes = (h <= 2) | ((h == 3) & ((x + dx) % 2 == side))
        k = blk_of(dx, h * (2 * side - 1))
        pl.when(goes)(lambda: act(half, k, 2 + side, start))

    def x_on(half, dy, start):
        even = (y + dy + NY) % 2 == 0
        pl.when(even)(lambda: act(half, blk_of(-1, dy), 0, start))
        pl.when(jnp.logical_not(even))(lambda: act(half, blk_of(1, dy), 1, start))

    send_all(0, me, (0, 1), True)
    send_all(1, me, (2, 3, 0, 1), True)
    send_all(0, me, (2, 3), True)

    tile = (lax.broadcasted_iota(I32, (rows, 128), 1) % rows == lax.broadcasted_iota(I32, (rows, 128), 0)).astype(F32)
    loads[2].wait()
    acol = jnp.concatenate([acol_ref[a] for a in range(per_row)], axis=0)
    spread = jnp.dot(acol.astype(F32), tile, preferred_element_type=F32, precision=EXACT)
    lane6 = lax.broadcasted_iota(I32, (per_row, 128), 1)
    mine6 = lane6 // rows == lax.broadcasted_iota(I32, (per_row, 128), 0)
    a_lane = jnp.sum(jnp.where(mine6, spread, 0.0), axis=0, keepdims=True)
    lane1 = lax.broadcasted_iota(I32, (1, 128), 1)
    a_lane = jnp.where(lane1 < rows * per_row, a_lane, -1.0)
    inner = lax.broadcasted_iota(I32, (n_inner, 128), 0).astype(F32)
    onehot = (inner == a_lane).astype(F32)
    before = (lax.broadcasted_iota(I32, (128, 128), 0) < lax.broadcasted_iota(I32, (128, 128), 1)).astype(BF16)
    count = jnp.dot(onehot.astype(BF16), before, preferred_element_type=F32)

    for dx in (1, -1):
        arrive(0, dx, 0)
        send_all(0, blk_of(dx, 0), (2, 3), True)
    x_on(0, 0, True)

    rank = jnp.sum(onehot * count, axis=0, keepdims=True)
    table = jnp.zeros((n_inner, 128), F32)
    lane_f = lane.astype(F32)
    for r in range(CAP):
        hit = jnp.where(count == float(r), onehot, 0.0)
        table = jnp.where(lane == r, jnp.sum(hit * lane_f, axis=1, keepdims=True), table)
    tab[...] = jnp.clip(table.astype(I32), 0, rows * per_row - 1)
    tab_copy = pltpu.make_async_copy(tab, tab_s, loc_sem.at[7])
    tab_copy.start()
    loads[3].wait()
    target = lax.dot_general(ccol_ref[...].astype(F32), tile, (((0,), (0,)), ((), ())), preferred_element_type=F32, precision=EXACT)
    prod[zero_block] = jnp.zeros((32, 128), F32)
    loads[5].wait()

    arrive(0, 2, 0)
    send_all(0, blk_of(2, 0), (2, 3), True)
    tab_copy.wait()

    def prepare(n, carry):
        a, i = n // rows, n % rows
        block = a_ref[a, i // 8, pl.ds(i % 8, 32, stride=8), :]
        high = block.astype(BF16).astype(F32)
        rest = block - high
        ap[n, 0:32, :] = jnp.where(low, high, pltpu.roll(rest, 64, 1)).astype(BF16)
        ap[n, 32:64, :] = jnp.where(low, pltpu.roll(high, 64, 1), rest).astype(BF16)
        return carry

    def products(k):
        right = jnp.concatenate([g0[k, 0:64, :], g1[k]], axis=1)
        high = right.astype(BF16)
        rest = (right - high.astype(F32)).astype(BF16)
        weights = jnp.concatenate([high, high, rest, rest], axis=0)
        left = jnp.concatenate([ap[tab_s[k, r]] for r in range(CAP)], axis=0)
        left = jnp.concatenate([left, left], axis=1)
        both = jnp.dot(left, weights, preferred_element_type=F32)
        for r in range(CAP):
            for pair in range(2):
                even = both[r * 64:r * 64 + 32, pair * 128:pair * 128 + 128]
                odd = both[r * 64 + 32:r * 64 + 64, pair * 128:pair * 128 + 128]
                prod[k * per_k + 2 * pair * CAP + r] = jnp.where(low, even, pltpu.roll(odd, 64, 1))
                prod[k * per_k + (2 * pair + 1) * CAP + r] = jnp.where(low, pltpu.roll(even, 64, 1), odd)

    def find_sources():
        def pick(k, cols):
            return jnp.where(a_lane == k.astype(F32), g0[k, 64:72, :], cols)

        cols = lax.fori_loop(0, n_inner, pick, jnp.full((8, 128), -1.0, F32), unroll=8)
        base = a_lane * float(per_k) + rank
        where_from = jnp.full((rows, 128), float(zero_block), F32)
        for s in range(4):
            where_from = jnp.where(target == cols[s:s + 1, :], base + float(CAP * s), where_from)
        off[...] = jnp.clip(where_from.astype(I32), 0, zero_block)
        pltpu.make_async_copy(off, off_s, loc_sem.at[8]).start()

    def gather_step(n, carry):
        h, u = n // NX + 1, n % NX
        dx = u + (u // 2) * (5 - 2 * u)
        older = (-(h - 1), (h - 1) * (1 - h // 5))
        pl.when(n == 4 * NX)(find_sources)

        for side in range(2):
            dy = h * (2 * side - 1)

            @pl.when(h <= 4 - side)
            def _():
                @pl.when(u == 0)
                def _():
                    arrive(1, 0, dy)
                    y_on(1, 0, h, side, True)
                    send_all(1, blk_of(0, dy), (0, 1), True)

                arrive(0, dx, dy)
                y_on(0, dx, h, side, True)

        for side in range(2):
            @pl.when((u == 0) & ((side == 0) | ((h >= 2) & (h <= 4))))
            def _():
                arrive(1, 1, older[side])
                arrive(1, -1, older[side])
                x_on(1, older[side], True)

        @pl.when(h == 1)
        def _():
            lax.fori_loop(0, 24, lambda j, carry: prepare(u * 24 + j, carry), 0, unroll=4)

        @pl.when(h >= 2)
        def _():
            @pl.when(u == 3)
            def _():
                for side in range(2):
                    arrive(1, 2, older[side])

            for side in range(2):
                products(blk_of(dx, older[side]))

        return carry

    lax.fori_loop(0, 5 * NX, gather_step, 0)
    pltpu.make_async_copy(off, off_s, loc_sem.at[8]).wait()

    def landed(m, i):
        total = prod[off_s[m, i]]
        for a in range(1, per_row):
            total = total + prod[off_s[m, a * rows + i]]
        return total

    def core_copy(part, delta):
        slot = part * NZ + delta % NZ
        return pltpu.make_async_remote_copy(
            src_ref=core_out.at[slot], dst_ref=core_in.at[slot],
            send_sem=core_send.at[slot], recv_sem=core_recv.at[slot],
            device_id=(me, sibling), device_id_type=MESH,
        )

    def give(part, delta):
        slot = part * NZ + delta % NZ
        m = (z + delta + NZ) % NZ * 2 + 1 - c

        def one(i, carry):
            core_out[slot, i] = landed(m, part * 8 + i)
            return carry

        lax.fori_loop(0, 8, one, 0, unroll=4)
        core_copy(part, delta).start()

    def z_copy(way, part, t):
        slot = (way * 2 + part) * 4 + t - 1
        source = core_in.at[part * NZ + z_delta(way, part, t) % NZ]
        return pltpu.make_async_remote_copy(
            src_ref=source, dst_ref=z_in.at[slot],
            send_sem=z_send.at[slot], recv_sem=z_recv.at[slot],
            device_id=(me, layer_of(1 - 2 * way)), device_id_type=MESH,
        )

    def z_steps(way, part):
        return 4 if way == part else 3

    def z_delta(way, part, t):
        return (z_steps(way, part) + 1 - t) * (1 - 2 * way)

    def pass_on(way, part, t):
        delta = z_delta(way, part, t)
        slot = part * NZ + delta % NZ
        m = (z + delta + NZ) % NZ * 2 + c
        core_copy(part, delta).wait_recv()
        if t > 1:
            z_copy(way, part, t - 1).wait_recv()

        def one(i, carry):
            total = landed(m, part * 8 + i) + core_in[slot, i]
            if t > 1:
                total = total + z_in[(way * 2 + part) * 4 + t - 2, i]
            core_in[slot, i] = total
            return carry

        lax.fori_loop(0, 8, one, 0, unroll=4)
        z_copy(way, part, t).start()

    def pieces(t):
        return [(way, part) for way, part in ((0, 0), (1, 1), (0, 1), (1, 0)) if t <= z_steps(way, part)]

    def give_all(t):
        if t <= 4:
            for way, part in pieces(t):
                give(part, z_delta(way, part, t))
        else:
            give(0, 0)
            give(1, 0)

    give_all(1)
    for t in range(1, 5):
        for way, part in pieces(t):
            pass_on(way, part, t)
        give_all(t + 1)

    loads[4].wait()
    loads[6].wait()
    for part in range(2):
        core_copy(part, 0).wait_recv()
        for way in range(2):
            z_copy(way, part, z_steps(way, part)).wait_recv()

        def one(n, carry):
            i = part * 8 + n
            total = landed(z * 2 + c, i) + core_in[part * NZ, n]
            for way in range(2):
                total = total + z_in[(way * 2 + part) * 4 + z_steps(way, part) - 1, n]
            out_ref[i] = keep_ref[0, i].astype(F32) * (1.5 * cval_ref[i] - 0.5 * total)
            return carry

        lax.fori_loop(0, 8, one, 0, unroll=4)

    send_all(0, me, (0, 1), False)
    x_on(0, 0, False)
    send_all(1, me, (2, 3, 0, 1), False)
    x_on(1, 0, False)
    for dx in range(NX):
        send_all(0, blk_of(dx, 0), (2, 3), False)

    def left(n, carry):
        h, u = n // NX + 1, n % NX
        for side in range(2):
            @pl.when(h <= 4 - side)
            def _():
                y_on(0, u, h, side, False)

                @pl.when(u == 0)
                def _():
                    y_on(1, 0, h, side, False)
                    send_all(1, blk_of(0, h * (2 * side - 1)), (0, 1), False)
                    x_on(1, h * (2 * side - 1), False)

        return carry

    lax.fori_loop(0, 4 * NX, left, 0)
    for part in range(2):
        for delta in range(NZ):
            core_copy(part, delta).wait_send()
    for t in range(1, 5):
        for way, part in pieces(t):
            z_copy(way, part, t).wait_send()


def body(a_vals, a_cols, b_vals, b_cols, c_cols, c_keep, c_vals):
    n_inner = NX * NY
    a = jnp.transpose(a_vals[0], (1, 0, 2)).reshape(6, 2, 8, 32, 128)
    a = jnp.transpose(a, (0, 1, 3, 2, 4)).reshape(6, 2, 256, 128)
    b = jnp.transpose(b_vals[0].reshape(4, 32, 128), (1, 0, 2)).reshape(128, 128)
    acol = jnp.transpose(a_cols, (2, 0, 1))
    hbm = pl.BlockSpec(memory_space=pltpu.HBM)
    vmem, smem, dma = pltpu.VMEM, pltpu.SMEM, pltpu.SemaphoreType.DMA
    out = pl.pallas_call(
        kernel,
        out_shape=jax.ShapeDtypeStruct((16, 32, 128), F32),
        in_specs=[hbm] * 7,
        out_specs=pl.BlockSpec(memory_space=pltpu.VMEM),
        scratch_shapes=[
            vmem((6, 2, 256, 128), F32),
            vmem((6, 1, 16), I32),
            vmem((128, 128), F32),
            smem((1, 4), I32),
            vmem((16, 16), I32),
            smem((1, 16), I32),
            vmem((16, 32, 128), F32),
            vmem((n_inner, 72, 128), F32),
            vmem((n_inner, 64, 128), F32),
            vmem((96, 64, 128), BF16),
            vmem((n_inner * 4 * CAP + 1, 32, 128), F32),
            vmem((n_inner, 128), I32),
            smem((n_inner, 128), I32),
            vmem((16, 128), I32),
            smem((16, 128), I32),
            vmem((16, 8, 32, 128), F32),
            vmem((16, 8, 32, 128), F32),
            vmem((16, 8, 32, 128), F32),
            dma((9,)),
            dma((2, 4, n_inner)),
            dma((2, n_inner)),
            dma((16,)),
            dma((16,)),
            dma((16,)),
            dma((16,)),
        ],
        compiler_params=pltpu.CompilerParams(
            collective_id=0, has_side_effects=True, vmem_limit_bytes=(64 << 20) - (64 << 10)
        ),
        cost_estimate=pl.CostEstimate(flops=1 << 31, bytes_accessed=8 << 20, transcendentals=0),
    )(a, acol, b, b_cols, c_cols, c_keep.T, c_vals.reshape(16, 32, 128))
    return out.reshape(16, 1, 4096)


def solution(mesh):
    in_specs = (
        P("layer", "blk", None, None),
        P("layer", "blk", None),
        P(("blk", "layer"), None, None),
        P(("blk", "layer"), None),
        P("blk", None),
        P("blk", "layer"),
        P("blk", "layer", None),
    )
    out_specs = P("blk", "layer", None)
    return jax.shard_map(body, mesh=mesh, in_specs=in_specs, out_specs=out_specs, check_vma=False)
```

time: 85.4 us -> 74.9 us (0.88)
  Pallas kernels: 78.9 us -> 73.1 us
  local copies, waits for them, and re-layouts: 4.29 us -> 1.67 us
  other arithmetic: 1.74 us -> 0 us
    pallas_call x1, Pallas kernels: 78.9 us -> 73.1 us  [body(): pl.pallas_call(kernel, out_shape=jax.ShapeDtypeStruct((16, 32, 128), F32)...]
    unnamed x11 -> x1, local copies, waits for them, and re-layouts: 4.29 us -> 1.67 us
    mul x3 -> x0, other arithmetic: 1.74 us -> none  [body(): return keep * (1.5 * c_vals - 0.5 * summed.reshape(16, 1, 4096))]
where the time goes in v2:
time: 74.9 us; the launch traced here: 74.7 us
  Pallas kernels  73.1 us (98%)
  local copies, waits for them, and re-layouts  1.67 us (2%)
    pallas_call x1, Pallas kernels, body(): pl.pallas_call(kernel, out_shape=jax.ShapeDtypeStruct((16, 32, 128), F32)...  73.1 us
    unnamed x1, local copies, waits for them, and re-layouts  1.67 us

profile of v2, /device:TPU:1, one launch (start us, length us, event | category | flops | bytes accessed | tf_op | source)
XLA Modules:
  0.0 74.7 jit_solution(5904319141147845010)
XLA Ops:
  0.0 73.1 %shard_map.73 = f32[16,32,128]{2,1,0:T(8,128)} custom-call(f32[6,2,256,128]{3,2,1,0:T(8,128)} %bitcast.19, s32[6,1,16]{2,1,0:T(1,128)} %bitcast.22, f32[128,128]{1,0:T(8,128)} %bitcast.21, s32[1,4]{1,0:T(1,128)} %bcol_hbm.1, s32[16,16]{1,0:T(8,128)} %ccol_hbm.1, s32[1,16]{1,0:T(1,128)} %bitcast.23, f32[16,32,128]{2,1,0:T(8,128)} %bitcast.20), custom_call_target="tpu_custom_call" | custom-call | flops 2147483648 | bytes 8388608 | tf_op jit(solution)/shard_map/pallas_call | solution.py:359
  73.1 1.7 %copy.11 = f32[16,1,4096]{2,1,0:T(1,128)} copy(f32[16,1,4096]{2,1,0:T(1,128)} %bitcast.18) | data formatting | bytes 524288

commit v3 on v2

v3 whole, which is shorter than its diff:
```python
import jax
import jax.numpy as jnp
from jax import lax
from jax.experimental import pallas as pl
from jax.experimental.pallas import tpu as pltpu
from jax.sharding import PartitionSpec as P

NX, NY, NZ = 4, 8, 8
SPLIT = 40
CAP = 6
MESH = pl.DeviceIdType.MESH
F32, BF16, I32 = jnp.float32, jnp.bfloat16, jnp.int32
EXACT = lax.Precision.HIGHEST


def kernel(
    a_hbm, acol_hbm, b_hbm, bcol_hbm, ccol_hbm, keep_hbm, cval_hbm, out_ref,
    a_ref, acol_ref, b_ref, bcol_ref, ccol_ref, keep_ref, cval_ref,
    g, ap, prod, tab, tab_s, off, off_s, core_out, core_in, z_in,
    loc_sem, ag_send, ag_recv, core_send, core_recv, z_send, z_recv,
):
    rows, per_row = 16, 6
    n_inner = NX * NY
    per_k = 4 * CAP
    zero_block = n_inner * per_k
    me, lay = lax.axis_index("blk"), lax.axis_index("layer")
    x, y = me // NY, me % NY
    z, c = lay // 2, lay % 2
    sibling = z * 2 + 1 - c

    def blk_of(dx, dy):
        return (x + dx + NX) % NX * NY + (y + dy + NY) % NY

    def layer_of(dz):
        return (z + dz + NZ) % NZ * 2 + c

    loads = [
        pltpu.make_async_copy(src, dst, loc_sem.at[n])
        for n, (src, dst) in enumerate((
            (b_hbm, b_ref), (bcol_hbm, bcol_ref), (acol_hbm, acol_ref), (ccol_hbm, ccol_ref),
            (keep_hbm, keep_ref), (a_hbm, a_ref), (cval_hbm, cval_ref),
        ))
    ]
    for load in loads:
        load.start()

    steps = ((1, 0), (-1, 0), (0, 1), (0, -1))
    barrier = pltpu.get_barrier_semaphore()
    for step in steps:
        pl.semaphore_signal(barrier, inc=1, device_id=(blk_of(*step), lay), device_id_type=MESH)
    for other in (sibling, layer_of(1), layer_of(-1)):
        pl.semaphore_signal(barrier, inc=1, device_id=(me, other), device_id_type=MESH)

    lane = lax.broadcasted_iota(I32, (32, 128), 1)
    low = lane < 64

    loads[0].wait()
    quarter = lane // 32
    blocks = [b_ref[pl.ds(s, 32, stride=4), :] for s in range(4)]
    for q in range(2):
        for parity in range(2):
            lines = blocks[0]
            for s in range(4):
                by = (s - 2 * parity - q) % 4 * 32
                moved = pltpu.roll(blocks[s], by, 1) if by else blocks[s]
                lines = moved if s == 0 else jnp.where(quarter == s, moved, lines)
            g[q, me, pl.ds(parity, 32, stride=2), :] = lines
    loads[1].wait()
    sub8 = lax.broadcasted_iota(I32, (8, 128), 0)
    meta = jnp.full((8, 128), -1, I32)
    for s in range(4):
        meta = jnp.where(sub8 == s, bcol_ref[0, s], meta)
    g[0, me, 64:72, :] = meta.astype(F32)

    pl.semaphore_wait(barrier, 7)

    def ag_copy(q, half, k, d):
        lines = pl.ds(0, SPLIT) if half == 1 else pl.ds(SPLIT, (72 if q == 0 else 64) - SPLIT)
        return pltpu.make_async_remote_copy(
            src_ref=g.at[q, k, lines], dst_ref=g.at[q, k, lines],
            send_sem=ag_send.at[q, half, d, k], recv_sem=ag_recv.at[q, half, k],
            device_id=(blk_of(*steps[d]), lay), device_id_type=MESH,
        )

    def act(q, half, k, d, start):
        if start:
            ag_copy(q, half, k, d).start()
        else:
            ag_copy(q, half, k, d).wait_send()

    def arrive(q, half, dx, dy):
        ag_copy(q, half, blk_of(dx, dy), 0).wait_recv()

    def send_all(q, half, k, ds, start):
        for d in ds:
            act(q, half, k, d, start)

    def y_on(q, half, dx, h, side, start):
        goes = (h <= 2) | ((h == 3) & ((x + dx) % 2 == side))
        k = blk_of(dx, h * (2 * side - 1))
        pl.when(goes)(lambda: act(q, half, k, 2 + side, start))

    def x_on(q, half, dy, start):
        even = (y + dy + NY) % 2 == 0
        pl.when(even)(lambda: act(q, half, blk_of(-1, dy), 0, start))
        pl.when(jnp.logical_not(even))(lambda: act(q, half, blk_of(1, dy), 1, start))

    def own(q, start):
        send_all(q, 0, me, (0, 1), start)
        send_all(q, 1, me, (2, 3, 0, 1), start)
        send_all(q, 0, me, (2, 3), start)

    def near(q):
        for dx in (1, -1):
            arrive(q, 0, dx, 0)
            send_all(q, 0, blk_of(dx, 0), (2, 3), True)
        x_on(q, 0, 0, True)

    def opposite(q):
        arrive(q, 0, 2, 0)
        send_all(q, 0, blk_of(2, 0), (2, 3), True)

    own(0, True)

    tile = (lax.broadcasted_iota(I32, (rows, 128), 1) % rows == lax.broadcasted_iota(I32, (rows, 128), 0)).astype(F32)
    loads[2].wait()
    acol = jnp.concatenate([acol_ref[a] for a in range(per_row)], axis=0)
    spread = jnp.dot(acol.astype(F32), tile, preferred_element_type=F32, precision=EXACT)
    lane6 = lax.broadcasted_iota(I32, (per_row, 128), 1)
    mine6 = lane6 // rows == lax.broadcasted_iota(I32, (per_row, 128), 0)
    a_lane = jnp.sum(jnp.where(mine6, spread, 0.0), axis=0, keepdims=True)
    lane1 = lax.broadcasted_iota(I32, (1, 128), 1)
    a_lane = jnp.where(lane1 < rows * per_row, a_lane, -1.0)
    inner = lax.broadcasted_iota(I32, (n_inner, 128), 0).astype(F32)
    onehot = (inner == a_lane).astype(F32)
    before = (lax.broadcasted_iota(I32, (128, 128), 0) < lax.broadcasted_iota(I32, (128, 128), 1)).astype(BF16)
    count = jnp.dot(onehot.astype(BF16), before, preferred_element_type=F32)

    near(0)

    rank = jnp.sum(onehot * count, axis=0, keepdims=True)
    table = jnp.zeros((n_inner, 128), F32)
    lane_f = lane.astype(F32)
    for r in range(CAP):
        hit = jnp.where(count == float(r), onehot, 0.0)
        table = jnp.where(lane == r, jnp.sum(hit * lane_f, axis=1, keepdims=True), table)
    tab[...] = jnp.clip(table.astype(I32), 0, rows * per_row - 1)
    tab_copy = pltpu.make_async_copy(tab, tab_s, loc_sem.at[7])
    tab_copy.start()
    loads[3].wait()
    target = lax.dot_general(ccol_ref[...].astype(F32), tile, (((0,), (0,)), ((), ())), preferred_element_type=F32, precision=EXACT)
    for q in range(2):
        prod[q, zero_block] = jnp.zeros((16, 128), F32)
    loads[5].wait()

    opposite(0)
    tab_copy.wait()

    def prepare(n, carry):
        a, i = n // rows, n % rows
        block = a_ref[a, i // 8, pl.ds(i % 8, 32, stride=8), :]
        high = block.astype(BF16).astype(F32)
        rest = block - high
        ap[n, 0:32, :] = jnp.where(low, high, pltpu.roll(rest, 64, 1)).astype(BF16)
        ap[n, 32:64, :] = jnp.where(low, pltpu.roll(high, 64, 1), rest).astype(BF16)
        return carry

    quarter16 = lax.broadcasted_iota(I32, (16, 128), 1) // 32

    def exchange(one, other, width):
        even = quarter16 // width % 2 == 0
        return (
            jnp.where(even, one, pltpu.roll(other, 32 * width, 1)),
            jnp.where(even, pltpu.roll(one, 128 - 32 * width, 1), other),
        )

    def products(q, k):
        right = g[q, k, 0:64, :]
        high = right.astype(BF16)
        rest = (right - high.astype(F32)).astype(BF16)
        weights = jnp.concatenate([high, high, rest, rest], axis=0)
        left = jnp.concatenate([ap[tab_s[k, r]] for r in range(CAP)], axis=0)
        left = jnp.concatenate([left, left], axis=1)
        both = jnp.dot(left, weights, preferred_element_type=F32)
        for r in range(CAP):
            w = [both[r * 64 + e * 16:r * 64 + e * 16 + 16, :] for e in range(4)]
            w[0], w[1] = exchange(w[0], w[1], 1)
            w[2], w[3] = exchange(w[2], w[3], 1)
            w[0], w[2] = exchange(w[0], w[2], 2)
            w[1], w[3] = exchange(w[1], w[3], 2)
            for s in range(4):
                prod[q, k * per_k + s * CAP + r] = w[s]

    def find_sources():
        def pick(k, cols):
            return jnp.where(a_lane == k.astype(F32), g[0, k, 64:72, :], cols)

        cols = lax.fori_loop(0, n_inner, pick, jnp.full((8, 128), -1.0, F32), unroll=8)
        base = a_lane * float(per_k) + rank
        where_from = jnp.full((rows, 128), float(zero_block), F32)
        for s in range(4):
            where_from = jnp.where(target == cols[s:s + 1, :], base + float(CAP * s), where_from)
        off[...] = jnp.clip(where_from.astype(I32), 0, zero_block)
        pltpu.make_async_copy(off, off_s, loc_sem.at[8]).start()

    def order(u):
        return u + (u // 2) * (5 - 2 * u)

    def gather_step(q, h, u):
        dx = order(u)
        older = (1 - h, h - 1)

        for side in range(2):
            dy = h * (2 * side - 1)

            @pl.when(h <= 4 - side)
            def _():
                @pl.when(u == 0)
                def _():
                    arrive(q, 1, 0, dy)
                    y_on(q, 1, 0, h, side, True)
                    send_all(q, 1, blk_of(0, dy), (0, 1), True)

                arrive(q, 0, dx, dy)
                y_on(q, 0, dx, h, side, True)

        for side in range(2):
            @pl.when((u == 0) & (h >= 1 + side))
            def _():
                arrive(q, 1, 1, older[side])
                arrive(q, 1, -1, older[side])
                x_on(q, 1, older[side], True)

        @pl.when(h >= 2)
        def _():
            @pl.when(u == 3)
            def _():
                for side in range(2):
                    arrive(q, 1, 2, older[side])

            for side in range(2):
                products(q, blk_of(dx, older[side]))

    def last_step(q, u):
        @pl.when(u == 0)
        def _():
            arrive(q, 1, 1, -4)
            arrive(q, 1, -1, -4)
            x_on(q, 1, -4, True)

        @pl.when(u == 3)
        def _():
            arrive(q, 1, 2, -4)
            arrive(q, 1, 2, 0)

        for dy in (-4, 0):
            products(q, blk_of(order(u), dy))

    def landed(q, m, i):
        total = prod[q, off_s[m, i]]
        for a in range(1, per_row):
            total = total + prod[q, off_s[m, a * rows + i]]
        return total

    def core_copy(q, part, delta):
        slot = part * NZ + delta % NZ
        return pltpu.make_async_remote_copy(
            src_ref=core_out.at[q, slot], dst_ref=core_in.at[q, slot],
            send_sem=core_send.at[q, slot], recv_sem=core_recv.at[q, slot],
            device_id=(me, sibling), device_id_type=MESH,
        )

    def give(q, part, delta):
        slot = part * NZ + delta % NZ
        m = (z + delta + NZ) % NZ * 2 + 1 - c

        def one(i, carry):
            core_out[q, slot, i] = landed(q, m, part * 8 + i)
            return carry

        lax.fori_loop(0, 8, one, 0, unroll=4)
        core_copy(q, part, delta).start()

    def z_copy(q, way, part, t):
        slot = (way * 2 + part) * 4 + t - 1
        source = core_in.at[q, part * NZ + z_delta(way, part, t) % NZ]
        return pltpu.make_async_remote_copy(
            src_ref=source, dst_ref=z_in.at[q, slot],
            send_sem=z_send.at[q, slot], recv_sem=z_recv.at[q, slot],
            device_id=(me, layer_of(1 - 2 * way)), device_id_type=MESH,
        )

    def z_steps(way, part):
        return 4 if way == part else 3

    def z_delta(way, part, t):
        return (z_steps(way, part) + 1 - t) * (1 - 2 * way)

    def pass_on(q, way, part, t):
        delta = z_delta(way, part, t)
        slot = part * NZ + delta % NZ
        m = (z + delta + NZ) % NZ * 2 + c
        core_copy(q, part, delta).wait_recv()
        if t > 1:
            z_copy(q, way, part, t - 1).wait_recv()

        def one(i, carry):
            total = landed(q, m, part * 8 + i) + core_in[q, slot, i]
            if t > 1:
                total = total + z_in[q, (way * 2 + part) * 4 + t - 2, i]
            core_in[q, slot, i] = total
            return carry

        lax.fori_loop(0, 8, one, 0, unroll=4)
        z_copy(q, way, part, t).start()

    def pieces(t):
        return [(way, part) for way, part in ((0, 0), (1, 1), (0, 1), (1, 0)) if t <= z_steps(way, part)]

    def give_all(q, t):
        if t <= 4:
            for way, part in pieces(t):
                give(q, part, z_delta(way, part, t))
        if t == 4:
            give(q, 0, 0)
            give(q, 1, 0)

    def pass_all(q, t, which):
        for way, part in pieces(t)[which]:
            pass_on(q, way, part, t)

    first, second = slice(0, 2), slice(2, 4)

    def gather_0(n, carry):
        h, u = n // NX + 1, n % NX

        @pl.when(h == 1)
        def _():
            lax.fori_loop(0, 24, lambda j, t: prepare(u * 24 + j, t), 0, unroll=4)

        gather_step(0, h, u)
        pl.when(n == 10)(lambda: own(1, True))
        pl.when(n == 13)(lambda: near(1))
        pl.when(n == 15)(lambda: opposite(1))
        return carry

    lax.fori_loop(0, 4 * NX, gather_0, 0)
    find_sources()

    def gather_1(n, carry):
        h, u = n // NX + 1, n % NX
        gather_step(1, h, u)
        pl.when(h == 1)(lambda: last_step(0, u))

        @pl.when(n == 4)
        def _():
            pltpu.make_async_copy(off, off_s, loc_sem.at[8]).wait()
            give_all(0, 1)

        pl.when(n == 5)(lambda: give_all(0, 2))
        pl.when(n == 6)(lambda: pass_all(0, 1, first))
        pl.when(n == 7)(lambda: pass_all(0, 1, second))
        pl.when(n == 8)(lambda: give_all(0, 3))
        pl.when(n == 10)(lambda: pass_all(0, 2, first))
        pl.when(n == 11)(lambda: pass_all(0, 2, second))
        pl.when(n == 12)(lambda: give_all(0, 4))
        pl.when(n == 14)(lambda: pass_all(0, 3, first))
        pl.when(n == 15)(lambda: pass_all(0, 3, second))
        return carry

    lax.fori_loop(0, 4 * NX, gather_1, 0)

    def finish_1(u, carry):
        last_step(1, u)
        return carry

    lax.fori_loop(0, NX, finish_1, 0)
    give_all(1, 1)
    pass_all(0, 4, first)
    for t in range(1, 5):
        give_all(1, t + 1)
        pass_all(1, t, slice(0, 4))

    loads[4].wait()
    loads[6].wait()
    for part in range(2):
        for q in range(2):
            core_copy(q, part, 0).wait_recv()
            for way in range(2):
                z_copy(q, way, part, z_steps(way, part)).wait_recv()

        def one(n, carry):
            i = part * 8 + n
            half = []
            for q in range(2):
                total = landed(q, z * 2 + c, i) + core_in[q, part * NZ, n]
                for way in range(2):
                    total = total + z_in[q, (way * 2 + part) * 4 + z_steps(way, part) - 1, n]
                half.append(total)
            keep = keep_ref[0, i].astype(F32)
            for lines, total in zip((pl.ds(0, 16), pl.ds(16, 16)), exchange(half[0], half[1], 1)):
                out_ref[i, lines, :] = keep * (1.5 * cval_ref[i, lines, :] - 0.5 * total)
            return carry

        lax.fori_loop(0, 8, one, 0, unroll=4)

    def left(n, carry):
        h, u = n // NX + 1, n % NX
        for q in range(2):
            for side in range(2):
                @pl.when(h <= 4 - side)
                def _():
                    y_on(q, 0, u, h, side, False)

                    @pl.when(u == 0)
                    def _():
                        dy = h * (2 * side - 1)
                        y_on(q, 1, 0, h, side, False)
                        send_all(q, 1, blk_of(0, dy), (0, 1), False)
                        x_on(q, 1, dy, False)

        return carry

    lax.fori_loop(0, 4 * NX, left, 0)
    for q in range(2):
        own(q, False)
        x_on(q, 0, 0, False)
        x_on(q, 1, 0, False)
        for dx in range(1, NX):
            send_all(q, 0, blk_of(dx, 0), (2, 3), False)
        for part in range(2):
            for delta in range(NZ):
                core_copy(q, part, delta).wait_send()
        for t in range(1, 5):
            for way, part in pieces(t):
                z_copy(q, way, part, t).wait_send()


def body(a_vals, a_cols, b_vals, b_cols, c_cols, c_keep, c_vals):
    n_inner = NX * NY
    a = jnp.transpose(a_vals[0], (1, 0, 2)).reshape(6, 2, 8, 32, 128)
    a = jnp.transpose(a, (0, 1, 3, 2, 4)).reshape(6, 2, 256, 128)
    b = jnp.transpose(b_vals[0].reshape(4, 32, 128), (1, 0, 2)).reshape(128, 128)
    acol = jnp.transpose(a_cols, (2, 0, 1))
    hbm = pl.BlockSpec(memory_space=pltpu.HBM)
    vmem, smem, dma = pltpu.VMEM, pltpu.SMEM, pltpu.SemaphoreType.DMA
    out = pl.pallas_call(
        kernel,
        out_shape=jax.ShapeDtypeStruct((16, 32, 128), F32),
        in_specs=[hbm] * 7,
        out_specs=pl.BlockSpec(memory_space=pltpu.VMEM),
        scratch_shapes=[
            vmem((6, 2, 256, 128), F32),
            vmem((6, 1, 16), I32),
            vmem((128, 128), F32),
            smem((1, 4), I32),
            vmem((16, 16), I32),
            smem((1, 16), I32),
            vmem((16, 32, 128), F32),
            vmem((2, n_inner, 72, 128), F32),
            vmem((96, 64, 128), BF16),
            vmem((2, n_inner * 4 * CAP + 1, 16, 128), F32),
            vmem((n_inner, 128), I32),
            smem((n_inner, 128), I32),
            vmem((16, 128), I32),
            smem((16, 128), I32),
            vmem((2, 16, 8, 16, 128), F32),
            vmem((2, 16, 8, 16, 128), F32),
            vmem((2, 16, 8, 16, 128), F32),
            dma((9,)),
            dma((2, 2, 4, n_inner)),
            dma((2, 2, n_inner)),
            dma((2, 16)),
            dma((2, 16)),
            dma((2, 16)),
            dma((2, 16)),
        ],
        compiler_params=pltpu.CompilerParams(
            collective_id=0, has_side_effects=True, vmem_limit_bytes=(64 << 20) - (64 << 10)
        ),
        cost_estimate=pl.CostEstimate(flops=1 << 31, bytes_accessed=8 << 20, transcendentals=0),
    )(a, acol, b, b_cols, c_cols, c_keep.T, c_vals.reshape(16, 32, 128))
    return out.reshape(16, 1, 4096)


def solution(mesh):
    in_specs = (
        P("layer", "blk", None, None),
        P("layer", "blk", None),
        P(("blk", "layer"), None, None),
        P(("blk", "layer"), None),
        P("blk", None),
        P("blk", "layer"),
        P("blk", "layer", None),
    )
    out_specs = P("blk", "layer", None)
    return jax.shard_map(body, mesh=mesh, in_specs=in_specs, out_specs=out_specs, check_vma=False)
```

time: 74.9 us -> 88.4 us (1.18); the launches traced: 74.7 us -> 87.3 us
  Pallas kernels: 73.1 us -> 85.6 us
    pallas_call x1, Pallas kernels: 73.1 us -> 85.6 us  [body(): pl.pallas_call(kernel, out_shape=jax.ShapeDtypeStruct((16, 32, 128), F32)...]
where the time goes in v3:
time: 88.4 us; the launch traced here: 87.3 us
  Pallas kernels  85.6 us (97%)
  local copies, waits for them, and re-layouts  1.67 us (2%)
    pallas_call x1, Pallas kernels, body(): pl.pallas_call(kernel, out_shape=jax.ShapeDtypeStruct((16, 32, 128), F32)...  85.6 us

profile of v3, /device:TPU:1, one launch (start us, length us, event | category | flops | bytes accessed | tf_op | source)
XLA Modules:
  0.0 87.3 jit_solution(16616294579257143857)
XLA Ops:
  0.0 85.6 %shard_map.73 = f32[16,32,128]{2,1,0:T(8,128)} custom-call(f32[6,2,256,128]{3,2,1,0:T(8,128)} %bitcast.19, s32[6,1,16]{2,1,0:T(1,128)} %bitcast.22, f32[128,128]{1,0:T(8,128)} %bitcast.21, s32[1,4]{1,0:T(1,128)} %bcol_hbm.1, s32[16,16]{1,0:T(8,128)} %ccol_hbm.1, s32[1,16]{1,0:T(1,128)} %bitcast.23, f32[16,32,128]{2,1,0:T(8,128)} %bitcast.20), custom_call_target="tpu_custom_call" | custom-call | flops 2147483648 | bytes 8388608 | tf_op jit(solution)/shard_map/pallas_call | solution.py:447
  85.6 1.7 %copy.11 = f32[16,1,4096]{2,1,0:T(1,128)} copy(f32[16,1,4096]{2,1,0:T(1,128)} %bitcast.18) | data formatting | bytes 524288

commit v4 on v2

v4 whole, which is shorter than its diff:
```python
import jax
import jax.numpy as jnp
from jax import lax
from jax.experimental import pallas as pl
from jax.experimental.pallas import tpu as pltpu
from jax.sharding import PartitionSpec as P

NX, NY, NZ = 4, 8, 8
CAP = 6
MESH = pl.DeviceIdType.MESH
F32, BF16, I32 = jnp.float32, jnp.bfloat16, jnp.int32
EXACT = lax.Precision.HIGHEST


def kernel(
    a_hbm, acol_hbm, b_hbm, bcol_hbm, ccol_hbm, keep_hbm, cval_hbm, out_ref,
    a_ref, acol_ref, b_ref, bcol_ref, ccol_ref, keep_ref, cval_ref,
    g0, g1, ap, prod, tab, tab_s, off, off_s, core_out, core_in, z_in,
    loc_sem, ag_send, g0_recv, g1_recv, core_send, core_recv, z_send, z_recv,
):
    rows, per_row = 16, 6
    n_inner = NX * NY
    per_k = 4 * CAP
    zero_block = n_inner * per_k
    me, lay = lax.axis_index("blk"), lax.axis_index("layer")
    x, y = me // NY, me % NY
    z, c = lay // 2, lay % 2
    sibling = z * 2 + 1 - c

    def blk_of(dx, dy):
        return (x + dx + NX) % NX * NY + (y + dy + NY) % NY

    def layer_of(dz):
        return (z + dz + NZ) % NZ * 2 + c

    loads = [
        pltpu.make_async_copy(src, dst, loc_sem.at[n])
        for n, (src, dst) in enumerate((
            (b_hbm, b_ref), (bcol_hbm, bcol_ref), (acol_hbm, acol_ref), (ccol_hbm, ccol_ref),
            (keep_hbm, keep_ref), (a_hbm, a_ref), (cval_hbm, cval_ref),
        ))
    ]
    for load in loads:
        load.start()

    steps = ((1, 0), (-1, 0), (0, 1), (0, -1))
    barrier = pltpu.get_barrier_semaphore()
    for step in steps:
        pl.semaphore_signal(barrier, inc=1, device_id=(blk_of(*step), lay), device_id_type=MESH)
    for other in (sibling, layer_of(1), layer_of(-1)):
        pl.semaphore_signal(barrier, inc=1, device_id=(me, other), device_id_type=MESH)

    lane = lax.broadcasted_iota(I32, (32, 128), 1)
    low = lane < 64

    loads[0].wait()
    for pair in range(2):
        first = b_ref[pl.ds(2 * pair, 32, stride=4), :]
        second = b_ref[pl.ds(2 * pair + 1, 32, stride=4), :]
        even = jnp.where(low, first, pltpu.roll(second, 64, 1))
        odd = jnp.where(low, pltpu.roll(first, 64, 1), second)
        g = g0 if pair == 0 else g1
        g[0, pl.ds(0, 32, stride=2), :] = even
        g[0, pl.ds(1, 32, stride=2), :] = odd
    loads[1].wait()
    sub8 = lax.broadcasted_iota(I32, (8, 128), 0)
    meta = jnp.full((8, 128), -1, I32)
    for s in range(4):
        meta = jnp.where(sub8 == s, bcol_ref[0, s], meta)
    g0[0, 64:72, :] = meta.astype(F32)

    pl.semaphore_wait(barrier, 7)

    def send(buf, recv, n, src, dst, d, count, lines=slice(None)):
        lines = pl.ds(*lines) if isinstance(lines, tuple) else lines
        pltpu.make_async_remote_copy(
            src_ref=buf.at[pl.ds(src, count), lines], dst_ref=buf.at[pl.ds(dst, count), lines],
            send_sem=ag_send.at[0 if buf is g0 else 1], recv_sem=recv.at[n],
            device_id=(blk_of(*steps[d]), lay), device_id_type=MESH,
        ).start()

    def arrive(buf, recv, n, place, count, lines=slice(None)):
        lines = pl.ds(*lines) if isinstance(lines, tuple) else lines
        piece = buf.at[pl.ds(place, count), lines]
        pltpu.make_async_copy(piece, piece, recv.at[n]).wait()

    def row0_on(part):
        src, count = ((0, 3), (3, 1))[part]
        for side in range(2):
            send(g0, g0_recv, 4 + 2 * (1 + side) + part, src, (1 + side) * NX + src, 2 + side, count)

    def x_pair(yi, count):
        for d in range(2):
            send(g1, g1_recv, 16 + 8 * (1 - d) + yi, yi, (2 - d) * NY + yi, d, count)

    def x_on(xi, yi):
        send(g1, g1_recv, 32 + yi, xi * NY + yi, 3 * NY + yi, 2 - xi, 1)

    for d in range(2):
        send(g0, g0_recv, 1 - d, 0, 2 - d, d, 1)
    for side in range(2):
        send(g1, g1_recv, 1 + side, 0, 1 + side, 2 + side, 1)
    x_pair(0, 1)

    tile = (lax.broadcasted_iota(I32, (rows, 128), 1) % rows == lax.broadcasted_iota(I32, (rows, 128), 0)).astype(F32)
    loads[2].wait()
    acol = jnp.concatenate([acol_ref[a] for a in range(per_row)], axis=0)
    spread = jnp.dot(acol.astype(F32), tile, preferred_element_type=F32, precision=EXACT)
    lane6 = lax.broadcasted_iota(I32, (per_row, 128), 1)
    mine6 = lane6 // rows == lax.broadcasted_iota(I32, (per_row, 128), 0)
    a_lane = jnp.sum(jnp.where(mine6, spread, 0.0), axis=0, keepdims=True)
    lane1 = lax.broadcasted_iota(I32, (1, 128), 1)
    a_lane = jnp.where(lane1 < rows * per_row, a_lane, -1.0)
    inner = lax.broadcasted_iota(I32, (n_inner, 128), 0).astype(F32)
    onehot = (inner == a_lane).astype(F32)
    before = (lax.broadcasted_iota(I32, (128, 128), 0) < lax.broadcasted_iota(I32, (128, 128), 1)).astype(BF16)
    count = jnp.dot(onehot.astype(BF16), before, preferred_element_type=F32)

    for xi in (1, 2):
        arrive(g0, g0_recv, xi - 1, xi, 1)
    send(g0, g0_recv, 2, 2, 3, 0, 1)
    row0_on(0)

    rank = jnp.sum(onehot * count, axis=0, keepdims=True)
    table = jnp.zeros((n_inner, 128), F32)
    lane_f = lane.astype(F32)
    for r in range(CAP):
        hit = jnp.where(count == float(r), onehot, 0.0)
        table = jnp.where(lane == r, jnp.sum(hit * lane_f, axis=1, keepdims=True), table)
    tab[...] = jnp.clip(table.astype(I32), 0, rows * per_row - 1)
    tab_copy = pltpu.make_async_copy(tab, tab_s, loc_sem.at[7])
    tab_copy.start()
    loads[3].wait()
    target = lax.dot_general(ccol_ref[...].astype(F32), tile, (((0,), (0,)), ((), ())), preferred_element_type=F32, precision=EXACT)
    prod[zero_block] = jnp.zeros((32, 128), F32)
    loads[5].wait()

    arrive(g0, g0_recv, 2, 3, 1)
    row0_on(1)
    tab_copy.wait()

    def prepare(n, carry):
        a, i = n // rows, n % rows
        block = a_ref[a, i // 8, pl.ds(i % 8, 32, stride=8), :]
        high = block.astype(BF16).astype(F32)
        rest = block - high
        ap[n, 0:32, :] = jnp.where(low, high, pltpu.roll(rest, 64, 1)).astype(BF16)
        ap[n, 32:64, :] = jnp.where(low, pltpu.roll(high, 64, 1), rest).astype(BF16)
        return carry

    def inner_at(xi, yi):
        dx = xi + xi // 2 * (5 - 2 * xi)
        dy = (yi + 1) // 2 * (1 - 2 * (yi % 2))
        return (x + dx) % NX * NY + (y + dy + NY) % NY

    def products(xi, yi):
        k = inner_at(xi, yi)
        right = jnp.concatenate([g0[yi * NX + xi, 0:64, :], g1[xi * NY + yi]], axis=1)
        high = right.astype(BF16)
        rest = (right - high.astype(F32)).astype(BF16)
        weights = jnp.concatenate([high, high, rest, rest], axis=0)
        left = jnp.concatenate([ap[tab_s[k, r]] for r in range(CAP)], axis=0)
        left = jnp.concatenate([left, left], axis=1)
        both = jnp.dot(left, weights, preferred_element_type=F32)
        for r in range(CAP):
            for pair in range(2):
                even = both[r * 64:r * 64 + 32, pair * 128:pair * 128 + 128]
                odd = both[r * 64 + 32:r * 64 + 64, pair * 128:pair * 128 + 128]
                prod[k * per_k + 2 * pair * CAP + r] = jnp.where(low, even, pltpu.roll(odd, 64, 1))
                prod[k * per_k + (2 * pair + 1) * CAP + r] = jnp.where(low, pltpu.roll(even, 64, 1), odd)

    def find_sources():
        def pick(k, cols):
            return jnp.where(a_lane == inner_at(k % NX, k // NX).astype(F32), g0[k, 64:72, :], cols)

        cols = lax.fori_loop(0, n_inner, pick, jnp.full((8, 128), -1.0, F32), unroll=8)
        base = a_lane * float(per_k) + rank
        where_from = jnp.full((rows, 128), float(zero_block), F32)
        for s in range(4):
            where_from = jnp.where(target == cols[s:s + 1, :], base + float(CAP * s), where_from)
        off[...] = jnp.clip(where_from.astype(I32), 0, zero_block)
        pltpu.make_async_copy(off, off_s, loc_sem.at[8]).start()

    def gather_step(h, carry):
        early, late = 2 * h - 1, 2 * h

        @pl.when(h <= 3)
        def _():
            for side, yi in ((0, early), (1, late)):
                arrive(g1, g1_recv, yi, yi, 1)

                @pl.when(h <= 2)
                def _():
                    send(g1, g1_recv, yi + 2, yi, yi + 2, 2 + side, 1)

                @pl.when(h == 3)
                def _():
                    send(g1, g1_recv, 7 + side, yi, 7, 2 + side, 1, (32 * side, 32))

            x_pair(early, 2)
            for side, yi in ((0, early), (1, late)):
                @pl.when(h == 1)
                def _():
                    arrive(g0, g0_recv, 4 + 2 * yi, yi * NX, 3)
                    arrive(g0, g0_recv, 5 + 2 * yi, yi * NX + 3, 1)

                @pl.when(h >= 2)
                def _():
                    arrive(g0, g0_recv, 4 + 2 * yi, yi * NX, NX)

                @pl.when(h <= 2)
                def _():
                    send(g0, g0_recv, 8 + 2 * yi, yi * NX, (yi + 2) * NX, 2 + side, NX)

                @pl.when(h == 3)
                def _():
                    send(g0, g0_recv, 18 + side, yi * NX + 2 * side, 7 * NX + 2 * side, 2 + side, 2)

        @pl.when(h == 4)
        def _():
            for side in range(2):
                arrive(g1, g1_recv, 7 + side, 7, 1, (32 * side, 32))
            x_pair(7, 1)
            for side in range(2):
                arrive(g0, g0_recv, 18 + side, 7 * NX + 2 * side, 2)

        @pl.when(h == 1)
        def _():
            for xi in (1, 2):
                arrive(g1, g1_recv, 8 + 8 * xi, xi * NY, 1)
            x_on(2, 0)
            lax.fori_loop(0, rows * per_row, prepare, 0, unroll=4)

        @pl.when((h >= 2) & (h <= 4))
        def _():
            for xi in (1, 2):
                arrive(g1, g1_recv, 8 + 8 * xi + 2 * h - 3, xi * NY + 2 * h - 3, 2)
            x_on(2, 2 * h - 3)
            x_on(1, 2 * h - 2)

        @pl.when(h == 5)
        def _():
            for xi in (1, 2):
                arrive(g1, g1_recv, 8 + 8 * xi + 7, xi * NY + 7, 1)
            x_on(1, 7)
            find_sources()

        @pl.when(h >= 2)
        def _():
            places = (2 * h - 3, (2 * h - 2) * (1 - h // 5))

            def pair(xi, carry):
                @pl.when(xi == 3)
                def _():
                    for yi in places:
                        arrive(g1, g1_recv, 32 + yi, 3 * NY + yi, 1)

                for yi in places:
                    products(xi, yi)
                return carry

            lax.fori_loop(0, NX, pair, 0)

        return carry

    lax.fori_loop(1, 6, gather_step, 0)
    pltpu.make_async_copy(off, off_s, loc_sem.at[8]).wait()

    def landed(m, i):
        total = prod[off_s[m, i]]
        for a in range(1, per_row):
            total = total + prod[off_s[m, a * rows + i]]
        return total

    def piece(n):
        t, j = n // 4 + 1, n % 4
        way, part = j % 2, (j + 1) // 2 % 2
        delta = (5 - j // 2 - t) * (1 - 2 * way)
        return t, way, part, (z + delta + NZ) % NZ

    def core_copy(n):
        return pltpu.make_async_remote_copy(
            src_ref=core_out.at[n], dst_ref=core_in.at[n],
            send_sem=core_send, recv_sem=core_recv.at[n],
            device_id=(me, sibling), device_id_type=MESH,
        )

    def z_copy(n, way):
        return pltpu.make_async_remote_copy(
            src_ref=core_in.at[n], dst_ref=z_in.at[n],
            send_sem=z_send, recv_sem=z_recv.at[n],
            device_id=(me, layer_of(1 - 2 * way)), device_id_type=MESH,
        )

    def give(n):
        _, _, part, to = piece(n)

        def one(i, carry):
            core_out[n, i] = landed(to * 2 + 1 - c, part * 8 + i)
            return carry

        lax.fori_loop(0, 8, one, 0, unroll=4)
        core_copy(n).start()

    def pass_on(n):
        t, way, part, to = piece(n)
        m = to * 2 + c
        core_copy(n).wait_recv()

        @pl.when(t == 1)
        def _():
            def one(i, carry):
                core_in[n, i] = landed(m, part * 8 + i) + core_in[n, i]
                return carry

            lax.fori_loop(0, 8, one, 0, unroll=4)

        @pl.when(t > 1)
        def _():
            z_copy(n - 4, way).wait_recv()

            def one(i, carry):
                core_in[n, i] = landed(m, part * 8 + i) + core_in[n, i] + z_in[n - 4, i]
                return carry

            lax.fori_loop(0, 8, one, 0, unroll=4)

        pl.when(n < 14)(lambda: z_copy(n, way).start())

    lag = 4

    def sum_step(n, carry):
        pl.when(n < 16)(lambda: give(n))
        pl.when(n >= lag)(lambda: pass_on(n - lag))
        return carry

    lax.fori_loop(0, 16 + lag, sum_step, 0)

    loads[4].wait()
    loads[6].wait()
    for part in range(2):
        z_copy(12 + part, 0).wait_recv()

        def one(n, carry):
            i = part * 8 + n
            total = core_in[15 - part, n] + z_in[12 + part, n]
            out_ref[i] = keep_ref[0, i].astype(F32) * (1.5 * cval_ref[i] - 0.5 * total)
            return carry

        lax.fori_loop(0, 8, one, 0, unroll=2)

    for n, buf in enumerate((g0, g1)):
        most = buf.at[pl.ds(0, n_inner - 1)]
        pltpu.make_async_copy(most, most, ag_send.at[n]).wait()
    pltpu.make_async_copy(core_out, core_out, core_send).wait()
    most = core_in.at[pl.ds(0, 14)]
    pltpu.make_async_copy(most, most, z_send).wait()


def body(a_vals, a_cols, b_vals, b_cols, c_cols, c_keep, c_vals):
    n_inner = NX * NY
    a = jnp.transpose(a_vals[0], (1, 0, 2)).reshape(6, 2, 8, 32, 128)
    a = jnp.transpose(a, (0, 1, 3, 2, 4)).reshape(6, 2, 256, 128)
    b = jnp.transpose(b_vals[0].reshape(4, 32, 128), (1, 0, 2)).reshape(128, 128)
    acol = jnp.transpose(a_cols, (2, 0, 1))
    hbm = pl.BlockSpec(memory_space=pltpu.HBM)
    vmem, smem, dma = pltpu.VMEM, pltpu.SMEM, pltpu.SemaphoreType.DMA
    out = pl.pallas_call(
        kernel,
        out_shape=jax.ShapeDtypeStruct((16, 32, 128), F32),
        in_specs=[hbm] * 7,
        out_specs=pl.BlockSpec(memory_space=pltpu.VMEM),
        scratch_shapes=[
            vmem((6, 2, 256, 128), F32),
            vmem((6, 1, 16), I32),
            vmem((128, 128), F32),
            smem((1, 4), I32),
            vmem((16, 16), I32),
            smem((1, 16), I32),
            vmem((16, 32, 128), F32),
            vmem((n_inner, 72, 128), F32),
            vmem((n_inner, 64, 128), F32),
            vmem((96, 64, 128), BF16),
            vmem((n_inner * 4 * CAP + 1, 32, 128), F32),
            vmem((n_inner, 128), I32),
            smem((n_inner, 128), I32),
            vmem((16, 128), I32),
            smem((16, 128), I32),
            vmem((16, 8, 32, 128), F32),
            vmem((16, 8, 32, 128), F32),
            vmem((16, 8, 32, 128), F32),
            dma((9,)),
            dma((2,)),
            dma((20,)),
            dma((40,)),
            dma,
            dma((16,)),
            dma,
            dma((14,)),
        ],
        compiler_params=pltpu.CompilerParams(
            collective_id=0, has_side_effects=True, vmem_limit_bytes=(64 << 20) - (64 << 10)
        ),
        cost_estimate=pl.CostEstimate(flops=1 << 31, bytes_accessed=8 << 20, transcendentals=0),
    )(a, acol, b, b_cols, c_cols, c_keep.T, c_vals.reshape(16, 32, 128))
    return out.reshape(16, 1, 4096)


def solution(mesh):
    in_specs = (
        P("layer", "blk", None, None),
        P("layer", "blk", None),
        P(("blk", "layer"), None, None),
        P(("blk", "layer"), None),
        P("blk", None),
        P("blk", "layer"),
        P("blk", "layer", None),
    )
    out_specs = P("blk", "layer", None)
    return jax.shard_map(body, mesh=mesh, in_specs=in_specs, out_specs=out_specs, check_vma=False)
```

time: 74.9 us -> 74.2 us (level)
  no operation moved by 1% of the time
where the time goes in v4:
time: 74.2 us; the launch traced here: 74.1 us
  Pallas kernels  72.4 us (98%)
  local copies, waits for them, and re-layouts  1.67 us (2%)
    pallas_call x1, Pallas kernels, body(): pl.pallas_call(kernel, out_shape=jax.ShapeDtypeStruct((16, 32, 128), F32)...  72.4 us
    unnamed x1, local copies, waits for them, and re-layouts  1.67 us

profile of v4, /device:TPU:1, one launch (start us, length us, event | category | flops | bytes accessed | tf_op | source)
XLA Modules:
  0.0 74.1 jit_solution(11070566555897624655)
XLA Ops:
  0.0 72.4 %shard_map.73 = f32[16,32,128]{2,1,0:T(8,128)} custom-call(f32[6,2,256,128]{3,2,1,0:T(8,128)} %bitcast.19, s32[6,1,16]{2,1,0:T(1,128)} %bitcast.22, f32[128,128]{1,0:T(8,128)} %bitcast.21, s32[1,4]{1,0:T(1,128)} %bcol_hbm.1, s32[16,16]{1,0:T(8,128)} %ccol_hbm.1, s32[1,16]{1,0:T(1,128)} %bitcast.23, f32[16,32,128]{2,1,0:T(8,128)} %bitcast.20), custom_call_target="tpu_custom_call" | custom-call | flops 2147483648 | bytes 8388608 | tf_op jit(solution)/shard_map/pallas_call | solution.py:368
  72.4 1.7 %copy.11 = f32[16,1,4096]{2,1,0:T(1,128)} copy(f32[16,1,4096]{2,1,0:T(1,128)} %bitcast.18) | data formatting | bytes 524288

commit v5 on v4

--- a/solution.py
+++ b/solution.py
@@ -6,6 +6,8 @@
 from jax.sharding import PartitionSpec as P
 
 NX, NY, NZ = 4, 8, 8
+TOP = 48
+PARTS = ((0, 1), (1, 2), (3, 1))
 CAP = 6
 MESH = pl.DeviceIdType.MESH
 F32, BF16, I32 = jnp.float32, jnp.bfloat16, jnp.int32
@@ -59,15 +61,18 @@
         second = b_ref[pl.ds(2 * pair + 1, 32, stride=4), :]
         even = jnp.where(low, first, pltpu.roll(second, 64, 1))
         odd = jnp.where(low, pltpu.roll(first, 64, 1), second)
-        g = g0 if pair == 0 else g1
-        g[0, pl.ds(0, 32, stride=2), :] = even
-        g[0, pl.ds(1, 32, stride=2), :] = odd
+        for parity, lines in ((0, even), (1, odd)):
+            if pair == 0:
+                g0[0, pl.ds(parity, TOP // 2, stride=2), :] = lines[:TOP // 2]
+                g1[0, pl.ds(64 + parity, 32 - TOP // 2, stride=2), :] = lines[TOP // 2:]
+            else:
+                g1[0, pl.ds(parity, 32, stride=2), :] = lines
     loads[1].wait()
     sub8 = lax.broadcasted_iota(I32, (8, 128), 0)
     meta = jnp.full((8, 128), -1, I32)
     for s in range(4):
         meta = jnp.where(sub8 == s, bcol_ref[0, s], meta)
-    g0[0, 64:72, :] = meta.astype(F32)
+    g0[0, TOP:TOP + 8, :] = meta.astype(F32)
 
     pl.semaphore_wait(barrier, 7)
 
@@ -85,9 +90,9 @@
         pltpu.make_async_copy(piece, piece, recv.at[n]).wait()
 
     def row0_on(part):
-        src, count = ((0, 3), (3, 1))[part]
+        src, count = PARTS[part]
         for side in range(2):
-            send(g0, g0_recv, 4 + 2 * (1 + side) + part, src, (1 + side) * NX + src, 2 + side, count)
+            send(g0, g0_recv, 3 * (1 + side) + part, src, (1 + side) * NX + src, 2 + side, count)
 
     def x_pair(yi, count):
         for d in range(2):
@@ -100,6 +105,7 @@
         send(g0, g0_recv, 1 - d, 0, 2 - d, d, 1)
     for side in range(2):
         send(g1, g1_recv, 1 + side, 0, 1 + side, 2 + side, 1)
+    row0_on(0)
     x_pair(0, 1)
 
     tile = (lax.broadcasted_iota(I32, (rows, 128), 1) % rows == lax.broadcasted_iota(I32, (rows, 128), 0)).astype(F32)
@@ -119,7 +125,7 @@
     for xi in (1, 2):
         arrive(g0, g0_recv, xi - 1, xi, 1)
     send(g0, g0_recv, 2, 2, 3, 0, 1)
-    row0_on(0)
+    row0_on(1)
 
     rank = jnp.sum(onehot * count, axis=0, keepdims=True)
     table = jnp.zeros((n_inner, 128), F32)
@@ -136,7 +142,7 @@
     loads[5].wait()
 
     arrive(g0, g0_recv, 2, 3, 1)
-    row0_on(1)
+    row0_on(2)
     tab_copy.wait()
 
     def prepare(n, carry):
@@ -155,7 +161,8 @@
 
     def products(xi, yi):
         k = inner_at(xi, yi)
-        right = jnp.concatenate([g0[yi * NX + xi, 0:64, :], g1[xi * NY + yi]], axis=1)
+        first = jnp.concatenate([g0[yi * NX + xi, 0:TOP, :], g1[xi * NY + yi, 64:128 - TOP, :]], axis=0)
+        right = jnp.concatenate([first, g1[xi * NY + yi, 0:64, :]], axis=1)
         high = right.astype(BF16)
         rest = (right - high.astype(F32)).astype(BF16)
         weights = jnp.concatenate([high, high, rest, rest], axis=0)
@@ -171,7 +178,7 @@
 
     def find_sources():
         def pick(k, cols):
-            return jnp.where(a_lane == inner_at(k % NX, k // NX).astype(F32), g0[k, 64:72, :], cols)
+            return jnp.where(a_lane == inner_at(k % NX, k // NX).astype(F32), g0[k, TOP:TOP + 8, :], cols)
 
         cols = lax.fori_loop(0, n_inner, pick, jnp.full((8, 128), -1.0, F32), unroll=8)
         base = a_lane * float(per_k) + rank
@@ -183,6 +190,7 @@
 
     def gather_step(h, carry):
         early, late = 2 * h - 1, 2 * h
+        half = (128 - TOP) // 2
 
         @pl.when(h <= 3)
         def _():
@@ -195,34 +203,25 @@
 
                 @pl.when(h == 3)
                 def _():
-                    send(g1, g1_recv, 7 + side, yi, 7, 2 + side, 1, (32 * side, 32))
+                    send(g1, g1_recv, 7 + side, yi, 7, 2 + side, 1, (half * side, half))
 
             x_pair(early, 2)
-            for side, yi in ((0, early), (1, late)):
-                @pl.when(h == 1)
-                def _():
-                    arrive(g0, g0_recv, 4 + 2 * yi, yi * NX, 3)
-                    arrive(g0, g0_recv, 5 + 2 * yi, yi * NX + 3, 1)
-
-                @pl.when(h >= 2)
-                def _():
-                    arrive(g0, g0_recv, 4 + 2 * yi, yi * NX, NX)
-
-                @pl.when(h <= 2)
-                def _():
-                    send(g0, g0_recv, 8 + 2 * yi, yi * NX, (yi + 2) * NX, 2 + side, NX)
-
-                @pl.when(h == 3)
-                def _():
-                    send(g0, g0_recv, 18 + side, yi * NX + 2 * side, 7 * NX + 2 * side, 2 + side, 2)
+            for part, (src, count) in enumerate(PARTS):
+                for side, yi in ((0, early), (1, late)):
+                    arrive(g0, g0_recv, 3 * yi + part, yi * NX + src, count)
+
+                    @pl.when(h <= (3 if (part == 1) == (side == 0) else 2))
+                    def _():
+                        to = yi + 2 - (h // 3 if side == 1 else 0)
+                        send(g0, g0_recv, 3 * to + part, yi * NX + src, to * NX + src, 2 + side, count)
 
         @pl.when(h == 4)
         def _():
             for side in range(2):
-                arrive(g1, g1_recv, 7 + side, 7, 1, (32 * side, 32))
+                arrive(g1, g1_recv, 7 + side, 7, 1, (half * side, half))
             x_pair(7, 1)
-            for side in range(2):
-                arrive(g0, g0_recv, 18 + side, 7 * NX + 2 * side, 2)
+            for part, (src, count) in enumerate(PARTS):
+                arrive(g0, g0_recv, 21 + part, 7 * NX + src, count)
 
         @pl.when(h == 1)
         def _():
@@ -327,7 +326,7 @@
 
         pl.when(n < 14)(lambda: z_copy(n, way).start())
 
-    lag = 4
+    lag = 3
 
     def sum_step(n, carry):
         pl.when(n < 16)(lambda: give(n))
@@ -378,8 +377,8 @@
             vmem((16, 16), I32),
             smem((1, 16), I32),
             vmem((16, 32, 128), F32),
-            vmem((n_inner, 72, 128), F32),
-            vmem((n_inner, 64, 128), F32),
+            vmem((n_inner, TOP + 8, 128), F32),
+            vmem((n_inner, 128 - TOP, 128), F32),
             vmem((96, 64, 128), BF16),
             vmem((n_inner * 4 * CAP + 1, 32, 128), F32),
             vmem((n_inner, 128), I32),
@@ -391,7 +390,7 @@
             vmem((16, 8, 32, 128), F32),
             dma((9,)),
             dma((2,)),
-            dma((20,)),
+            dma((24,)),
             dma((40,)),
             dma,
             dma((16,)),

time: 74.2 us -> 72.9 us (0.982)
  Pallas kernels: 72.4 us -> 71.1 us
    pallas_call x1, Pallas kernels: 72.4 us -> 71.1 us  [body(): pl.pallas_call(kernel, out_shape=jax.ShapeDtypeStruct((16, 32, 128), F32)...]
where the time goes in v5:
time: 72.9 us; the launch traced here: 72.8 us
  Pallas kernels  71.1 us (98%)
  local copies, waits for them, and re-layouts  1.67 us (2%)
    pallas_call x1, Pallas kernels, body(): pl.pallas_call(kernel, out_shape=jax.ShapeDtypeStruct((16, 32, 128), F32)...  71.1 us
    unnamed x1, local copies, waits for them, and re-layouts  1.67 us

profile of v5, /device:TPU:1, one launch (start us, length us, event | category | flops | bytes accessed | tf_op | source)
XLA Modules:
  0.0 72.8 jit_solution(49113688774134189)
XLA Ops:
  0.0 71.1 %shard_map.73 = f32[16,32,128]{2,1,0:T(8,128)} custom-call(f32[6,2,256,128]{3,2,1,0:T(8,128)} %bitcast.19, s32[6,1,16]{2,1,0:T(1,128)} %bitcast.22, f32[128,128]{1,0:T(8,128)} %bitcast.21, s32[1,4]{1,0:T(1,128)} %bcol_hbm.1, s32[16,16]{1,0:T(8,128)} %ccol_hbm.1, s32[1,16]{1,0:T(1,128)} %bitcast.23, f32[16,32,128]{2,1,0:T(8,128)} %bitcast.20), custom_call_target="tpu_custom_call" | custom-call | flops 2147483648 | bytes 8388608 | tf_op jit(solution)/shard_map/pallas_call | solution.py:367
  71.1 1.7 %copy.11 = f32[16,1,4096]{2,1,0:T(1,128)} copy(f32[16,1,4096]{2,1,0:T(1,128)} %bitcast.18) | data formatting | bytes 524288

commit v6 on v5

--- a/solution.py
+++ b/solution.py
@@ -145,13 +145,16 @@
     row0_on(2)
     tab_copy.wait()
 
-    def prepare(n, carry):
-        a, i = n // rows, n % rows
-        block = a_ref[a, i // 8, pl.ds(i % 8, 32, stride=8), :]
-        high = block.astype(BF16).astype(F32)
-        rest = block - high
-        ap[n, 0:32, :] = jnp.where(low, high, pltpu.roll(rest, 64, 1)).astype(BF16)
-        ap[n, 32:64, :] = jnp.where(low, pltpu.roll(high, 64, 1), rest).astype(BF16)
+    def prepare(group, carry):
+        blocks = []
+        for n in range(4):
+            a, i = group // 4, group % 4 * 4 + n
+            blocks.append(a_ref[a, i // 8, pl.ds(i % 8, 32, stride=8), :])
+        for n, block in enumerate(blocks):
+            high = block.astype(BF16).astype(F32)
+            rest = block - high
+            ap[group * 4 + n, 0:32, :] = jnp.where(low, high, pltpu.roll(rest, 64, 1)).astype(BF16)
+            ap[group * 4 + n, 32:64, :] = jnp.where(low, pltpu.roll(high, 64, 1), rest).astype(BF16)
         return carry
 
     def inner_at(xi, yi):
@@ -159,7 +162,7 @@
         dy = (yi + 1) // 2 * (1 - 2 * (yi % 2))
         return (x + dx) % NX * NY + (y + dy + NY) % NY
 
-    def products(xi, yi):
+    def factors(xi, yi):
         k = inner_at(xi, yi)
         first = jnp.concatenate([g0[yi * NX + xi, 0:TOP, :], g1[xi * NY + yi, 64:128 - TOP, :]], axis=0)
         right = jnp.concatenate([first, g1[xi * NY + yi, 0:64, :]], axis=1)
@@ -167,14 +170,21 @@
         rest = (right - high.astype(F32)).astype(BF16)
         weights = jnp.concatenate([high, high, rest, rest], axis=0)
         left = jnp.concatenate([ap[tab_s[k, r]] for r in range(CAP)], axis=0)
-        left = jnp.concatenate([left, left], axis=1)
-        both = jnp.dot(left, weights, preferred_element_type=F32)
+        return k, jnp.concatenate([left, left], axis=1), weights
+
+    def keep_products(k, both):
         for r in range(CAP):
             for pair in range(2):
                 even = both[r * 64:r * 64 + 32, pair * 128:pair * 128 + 128]
                 odd = both[r * 64 + 32:r * 64 + 64, pair * 128:pair * 128 + 128]
                 prod[k * per_k + 2 * pair * CAP + r] = jnp.where(low, even, pltpu.roll(odd, 64, 1))
                 prod[k * per_k + (2 * pair + 1) * CAP + r] = jnp.where(low, pltpu.roll(even, 64, 1), odd)
+
+    def products(xi, places):
+        both = [factors(xi, yi) for yi in places]
+        both = [(k, jnp.dot(left, weights, preferred_element_type=F32)) for k, left, weights in both]
+        for k, values in both:
+            keep_products(k, values)
 
     def find_sources():
         def pick(k, cols):
@@ -228,7 +238,7 @@
             for xi in (1, 2):
                 arrive(g1, g1_recv, 8 + 8 * xi, xi * NY, 1)
             x_on(2, 0)
-            lax.fori_loop(0, rows * per_row, prepare, 0, unroll=4)
+            lax.fori_loop(0, rows * per_row // 4, prepare, 0, unroll=2)
 
         @pl.when((h >= 2) & (h <= 4))
         def _():
@@ -254,8 +264,7 @@
                     for yi in places:
                         arrive(g1, g1_recv, 32 + yi, 3 * NY + yi, 1)
 
-                for yi in places:
-                    products(xi, yi)
+                products(xi, places)
                 return carry
 
             lax.fori_loop(0, NX, pair, 0)
@@ -272,10 +281,11 @@
         return total
 
     def piece(n):
-        t, j = n // 4 + 1, n % 4
-        way, part = j % 2, (j + 1) // 2 % 2
-        delta = (5 - j // 2 - t) * (1 - 2 * way)
-        return t, way, part, (z + delta + NZ) % NZ
+        t, j = n // 8 + 1, n % 8
+        way = j % 2
+        row = (way + j // 4) % 2 * 8 + j // 2 % 2 * 4
+        delta = (5 - j // 4 - t) * (1 - 2 * way)
+        return t, way, row, (z + delta + NZ) % NZ
 
     def core_copy(n):
         return pltpu.make_async_remote_copy(
@@ -292,67 +302,55 @@
         )
 
     def give(n):
-        _, _, part, to = piece(n)
-
-        def one(i, carry):
-            core_out[n, i] = landed(to * 2 + 1 - c, part * 8 + i)
-            return carry
-
-        lax.fori_loop(0, 8, one, 0, unroll=4)
+        _, _, row, to = piece(n)
+        sums = [landed(to * 2 + 1 - c, row + i) for i in range(4)]
+        for i in range(4):
+            core_out[n, i] = sums[i]
         core_copy(n).start()
 
     def pass_on(n):
-        t, way, part, to = piece(n)
-        m = to * 2 + c
+        t, way, row, to = piece(n)
         core_copy(n).wait_recv()
 
         @pl.when(t == 1)
         def _():
-            def one(i, carry):
-                core_in[n, i] = landed(m, part * 8 + i) + core_in[n, i]
-                return carry
-
-            lax.fori_loop(0, 8, one, 0, unroll=4)
+            sums = [landed(to * 2 + c, row + i) + core_in[n, i] for i in range(4)]
+            for i in range(4):
+                core_in[n, i] = sums[i]
 
         @pl.when(t > 1)
         def _():
-            z_copy(n - 4, way).wait_recv()
-
-            def one(i, carry):
-                core_in[n, i] = landed(m, part * 8 + i) + core_in[n, i] + z_in[n - 4, i]
-                return carry
-
-            lax.fori_loop(0, 8, one, 0, unroll=4)
-
-        pl.when(n < 14)(lambda: z_copy(n, way).start())
-
-    lag = 3
+            z_copy(n - 8, way).wait_recv()
+            sums = [landed(to * 2 + c, row + i) + core_in[n, i] + z_in[n - 8, i] for i in range(4)]
+            for i in range(4):
+                core_in[n, i] = sums[i]
+
+        pl.when(n < 28)(lambda: z_copy(n, way).start())
+
+    lag = 6
 
     def sum_step(n, carry):
-        pl.when(n < 16)(lambda: give(n))
+        pl.when(n < 32)(lambda: give(n))
         pl.when(n >= lag)(lambda: pass_on(n - lag))
         return carry
 
-    lax.fori_loop(0, 16 + lag, sum_step, 0)
+    lax.fori_loop(0, 32 + lag, sum_step, 0)
 
     loads[4].wait()
     loads[6].wait()
-    for part in range(2):
-        z_copy(12 + part, 0).wait_recv()
-
-        def one(n, carry):
-            i = part * 8 + n
-            total = core_in[15 - part, n] + z_in[12 + part, n]
-            out_ref[i] = keep_ref[0, i].astype(F32) * (1.5 * cval_ref[i] - 0.5 * total)
-            return carry
-
-        lax.fori_loop(0, 8, one, 0, unroll=2)
+    for n in range(24, 28):
+        mine = n + 5 - n % 2 * 2
+        row = (1 - n % 2 + 1) % 2 * 8 + n // 2 % 2 * 4
+        z_copy(n, 0).wait_recv()
+        for i in range(4):
+            total = core_in[mine, i] + z_in[n, i]
+            out_ref[row + i] = keep_ref[0, row + i].astype(F32) * (1.5 * cval_ref[row + i] - 0.5 * total)
 
     for n, buf in enumerate((g0, g1)):
         most = buf.at[pl.ds(0, n_inner - 1)]
         pltpu.make_async_copy(most, most, ag_send.at[n]).wait()
     pltpu.make_async_copy(core_out, core_out, core_send).wait()
-    most = core_in.at[pl.ds(0, 14)]
+    most = core_in.at[pl.ds(0, 28)]
     pltpu.make_async_copy(most, most, z_send).wait()
 
 
@@ -385,17 +383,17 @@
             smem((n_inner, 128), I32),
             vmem((16, 128), I32),
             smem((16, 128), I32),
-            vmem((16, 8, 32, 128), F32),
-            vmem((16, 8, 32, 128), F32),
-            vmem((16, 8, 32, 128), F32),
+            vmem((32, 4, 32, 128), F32),
+            vmem((32, 4, 32, 128), F32),
+            vmem((32, 4, 32, 128), F32),
             dma((9,)),
             dma((2,)),
             dma((24,)),
             dma((40,)),
             dma,
-            dma((16,)),
+            dma((32,)),
             dma,
-            dma((14,)),
+            dma((28,)),
         ],
         compiler_params=pltpu.CompilerParams(
             collective_id=0, has_side_effects=True, vmem_limit_bytes=(64 << 20) - (64 << 10)

time: 72.9 us -> 72 us (0.988)
  Pallas kernels: 71.1 us -> 70.1 us
    pallas_call x1, Pallas kernels: 71.1 us -> 70.1 us  [body(): pl.pallas_call(kernel, out_shape=jax.ShapeDtypeStruct((16, 32, 128), F32)...]
where the time goes in v6:
time: 72 us; the launch traced here: 71.8 us
  Pallas kernels  70.1 us (97%)
  local copies, waits for them, and re-layouts  1.67 us (2%)
    pallas_call x1, Pallas kernels, body(): pl.pallas_call(kernel, out_shape=jax.ShapeDtypeStruct((16, 32, 128), F32)...  70.1 us
    unnamed x1, local copies, waits for them, and re-layouts  1.67 us

profile of v6, /device:TPU:1, one launch (start us, length us, event | category | flops | bytes accessed | tf_op | source)
XLA Modules:
  0.0 71.8 jit_solution(2856551320594435207)
XLA Ops:
  0.0 70.1 %shard_map.73 = f32[16,32,128]{2,1,0:T(8,128)} custom-call(f32[6,2,256,128]{3,2,1,0:T(8,128)} %bitcast.19, s32[6,1,16]{2,1,0:T(1,128)} %bitcast.22, f32[128,128]{1,0:T(8,128)} %bitcast.21, s32[1,4]{1,0:T(1,128)} %bcol_hbm.1, s32[16,16]{1,0:T(8,128)} %ccol_hbm.1, s32[1,16]{1,0:T(1,128)} %bitcast.23, f32[16,32,128]{2,1,0:T(8,128)} %bitcast.20), custom_call_target="tpu_custom_call" | custom-call | flops 2147483648 | bytes 8388608 | tf_op jit(solution)/shard_map/pallas_call | solution.py:365
  70.2 1.7 %copy.11 = f32[16,1,4096]{2,1,0:T(1,128)} copy(f32[16,1,4096]{2,1,0:T(1,128)} %bitcast.18) | data formatting | bytes 524288

commit v7 on v6

--- a/solution.py
+++ b/solution.py
@@ -11,7 +11,6 @@
 CAP = 6
 MESH = pl.DeviceIdType.MESH
 F32, BF16, I32 = jnp.float32, jnp.bfloat16, jnp.int32
-EXACT = lax.Precision.HIGHEST
 
 
 def kernel(
@@ -35,6 +34,13 @@
     def layer_of(dz):
         return (z + dz + NZ) % NZ * 2 + c
 
+    steps = ((1, 0), (-1, 0), (0, 1), (0, -1))
+    barrier = pltpu.get_barrier_semaphore()
+    for step in steps:
+        pl.semaphore_signal(barrier, inc=1, device_id=(blk_of(*step), lay), device_id_type=MESH)
+    for other in (sibling, layer_of(1), layer_of(-1)):
+        pl.semaphore_signal(barrier, inc=1, device_id=(me, other), device_id_type=MESH)
+
     loads = [
         pltpu.make_async_copy(src, dst, loc_sem.at[n])
         for n, (src, dst) in enumerate((
@@ -44,13 +50,6 @@
     ]
     for load in loads:
         load.start()
-
-    steps = ((1, 0), (-1, 0), (0, 1), (0, -1))
-    barrier = pltpu.get_barrier_semaphore()
-    for step in steps:
-        pl.semaphore_signal(barrier, inc=1, device_id=(blk_of(*step), lay), device_id_type=MESH)
-    for other in (sibling, layer_of(1), layer_of(-1)):
-        pl.semaphore_signal(barrier, inc=1, device_id=(me, other), device_id_type=MESH)
 
     lane = lax.broadcasted_iota(I32, (32, 128), 1)
     low = lane < 64
@@ -108,10 +107,10 @@
     row0_on(0)
     x_pair(0, 1)
 
-    tile = (lax.broadcasted_iota(I32, (rows, 128), 1) % rows == lax.broadcasted_iota(I32, (rows, 128), 0)).astype(F32)
+    tile = (lax.broadcasted_iota(I32, (rows, 128), 1) % rows == lax.broadcasted_iota(I32, (rows, 128), 0)).astype(BF16)
     loads[2].wait()
     acol = jnp.concatenate([acol_ref[a] for a in range(per_row)], axis=0)
-    spread = jnp.dot(acol.astype(F32), tile, preferred_element_type=F32, precision=EXACT)
+    spread = jnp.dot(acol.astype(F32).astype(BF16), tile, preferred_element_type=F32)
     lane6 = lax.broadcasted_iota(I32, (per_row, 128), 1)
     mine6 = lane6 // rows == lax.broadcasted_iota(I32, (per_row, 128), 0)
     a_lane = jnp.sum(jnp.where(mine6, spread, 0.0), axis=0, keepdims=True)
@@ -137,13 +136,15 @@
     tab_copy = pltpu.make_async_copy(tab, tab_s, loc_sem.at[7])
     tab_copy.start()
     loads[3].wait()
-    target = lax.dot_general(ccol_ref[...].astype(F32), tile, (((0,), (0,)), ((), ())), preferred_element_type=F32, precision=EXACT)
+    ccol = ccol_ref[...]
+    digits = jnp.concatenate([ccol // 16, ccol % 16], axis=1).astype(F32).astype(BF16)
+    digits = lax.dot_general(digits, tile, (((0,), (0,)), ((), ())), preferred_element_type=F32)
+    target = digits[:rows] * 16.0 + digits[rows:]
     prod[zero_block] = jnp.zeros((32, 128), F32)
     loads[5].wait()
 
     arrive(g0, g0_recv, 2, 3, 1)
     row0_on(2)
-    tab_copy.wait()
 
     def prepare(group, carry):
         blocks = []
@@ -151,10 +152,10 @@
             a, i = group // 4, group % 4 * 4 + n
             blocks.append(a_ref[a, i // 8, pl.ds(i % 8, 32, stride=8), :])
         for n, block in enumerate(blocks):
-            high = block.astype(BF16).astype(F32)
-            rest = block - high
-            ap[group * 4 + n, 0:32, :] = jnp.where(low, high, pltpu.roll(rest, 64, 1)).astype(BF16)
-            ap[group * 4 + n, 32:64, :] = jnp.where(low, pltpu.roll(high, 64, 1), rest).astype(BF16)
+            turned = pltpu.roll(block, 64, 1)
+            for parity, twice in enumerate((jnp.where(low, block, turned), jnp.where(low, turned, block))):
+                high = twice.astype(BF16).astype(F32)
+                ap[group * 4 + n, 32 * parity:32 * parity + 32, :] = jnp.where(low, high, twice - high).astype(BF16)
         return carry
 
     def inner_at(xi, yi):
@@ -177,8 +178,9 @@
             for pair in range(2):
                 even = both[r * 64:r * 64 + 32, pair * 128:pair * 128 + 128]
                 odd = both[r * 64 + 32:r * 64 + 64, pair * 128:pair * 128 + 128]
-                prod[k * per_k + 2 * pair * CAP + r] = jnp.where(low, even, pltpu.roll(odd, 64, 1))
-                prod[k * per_k + (2 * pair + 1) * CAP + r] = jnp.where(low, pltpu.roll(even, 64, 1), odd)
+                moved = pltpu.roll(jnp.where(low, odd, even), 64, 1)
+                prod[k * per_k + 2 * pair * CAP + r] = jnp.where(low, even, moved)
+                prod[k * per_k + (2 * pair + 1) * CAP + r] = jnp.where(low, moved, odd)
 
     def products(xi, places):
         both = [factors(xi, yi) for yi in places]
@@ -256,6 +258,7 @@
 
         @pl.when(h >= 2)
         def _():
+            pl.when(h == 2)(tab_copy.wait)
             places = (2 * h - 3, (2 * h - 2) * (1 - h // 5))
 
             def pair(xi, carry):

time: 72 us -> 71.6 us (level)
  no operation moved by 1% of the time
where the time goes in v7:
time: 71.6 us; the launch traced here: 71.4 us
  Pallas kernels  69.8 us (97%)
  local copies, waits for them, and re-layouts  1.67 us (2%)
    pallas_call x1, Pallas kernels, body(): pl.pallas_call(kernel, out_shape=jax.ShapeDtypeStruct((16, 32, 128), F32)...  69.8 us
    unnamed x1, local copies, waits for them, and re-layouts  1.67 us

profile of v7, /device:TPU:1, one launch (start us, length us, event | category | flops | bytes accessed | tf_op | source)
XLA Modules:
  0.0 71.4 jit_solution(6322953192542837363)
XLA Ops:
  0.0 69.8 %shard_map.73 = f32[16,32,128]{2,1,0:T(8,128)} custom-call(f32[6,2,256,128]{3,2,1,0:T(8,128)} %bitcast.19, s32[6,1,16]{2,1,0:T(1,128)} %bitcast.22, f32[128,128]{1,0:T(8,128)} %bitcast.21, s32[1,4]{1,0:T(1,128)} %bcol_hbm.1, s32[16,16]{1,0:T(8,128)} %ccol_hbm.1, s32[1,16]{1,0:T(1,128)} %bitcast.23, f32[16,32,128]{2,1,0:T(8,128)} %bitcast.20), custom_call_target="tpu_custom_call" | custom-call | flops 2147483648 | bytes 8388608 | tf_op jit(solution)/shard_map/pallas_call | solution.py:368
  69.8 1.7 %copy.11 = f32[16,1,4096]{2,1,0:T(1,128)} copy(f32[16,1,4096]{2,1,0:T(1,128)} %bitcast.18) | data formatting | bytes 524288
